TPU v7x, 128 devices: a whole 4x4x4 slice. The times are simulated.
128 devices in a mesh: grp: 4 (over x), seq: 32 (over z, y, core).
Axes of the slice: x: 4, y: 4, z: 4, core: 2. Of those that a mesh axis runs over, the one named last changes fastest.
Arguments:
- queries: bfloat16 [32768, 2048], P(('grp', 'seq')), may hold values from -150 to 150
- key_states: bfloat16 [32768, 2048], P(('grp', 'seq')), may hold values from -6 to 6
- value_states: bfloat16 [32768, 2048], P(('grp', 'seq')), may hold values from -6 to 6
- attn_out: bfloat16 [32768, 2048], P(('grp', 'seq')), may hold values from -6 to 6
- out_grad: bfloat16 [32768, 2048], P(('grp', 'seq')), may hold values from -6 to 6
- owner_ids: int32 [4, 16], replicated, may hold values from 0 to 31, as said below
Outputs:
- query_grad: bfloat16 [32768, 2048], P(('grp', 'seq'))
- key_grad: bfloat16 [32768, 2048], P(('grp', 'seq'))
- value_grad: bfloat16 [32768, 2048], P(('grp', 'seq'))
Inputs may be any that keep to these rules, and one draw needn't show every extreme that they name: In each group the owners never decrease along the blocks (owner_ids[g, b] <= owner_ids[g, b + 1]), so a shard's blocks are consecutive; every shard holds at most 2 blocks, and in every group some shard holds exactly 2.
All inputs are finite; a program needn't handle non-finite values.
Results may differ from a plain program's by a relative error of at most 0.005.
Values may be sent and summed in bfloat16 or wider, within the bound.
A program may use at most 128 MiB of HBM per device.

v0:
```python
import jax
import jax.numpy as jnp
from jax import lax
from jax.sharding import PartitionSpec as P

HD = 128
BLK = 128
HOPS = 3


def passed_along(array, axis, by):
    size = lax.axis_size(axis)
    pairs = [(i, i + by) for i in range(size) if 0 <= i + by < size]
    return lax.ppermute(array, axis, pairs)


def live_rows(count, row_count):
    block_idx = jnp.arange(row_count, dtype=jnp.int32) // BLK
    return block_idx < count


def log_total(scores, allowed):
    masked = jnp.where(allowed, scores, -1e30)
    row_max = jnp.max(masked, axis=-1, keepdims=True)
    return row_max[..., 0] + jnp.log(jnp.sum(jnp.exp(masked - row_max), axis=-1))


def pair_products(first_op, second_op, head_count):
    return jnp.einsum(
        "ihd,jhd->hij",
        first_op.reshape(first_op.shape[0], head_count, HD),
        second_op.reshape(second_op.shape[0], head_count, HD),
        preferred_element_type=jnp.float32,
    )


def grad_terms(scores, log_sum, allowed, prob_grad, row_delta):
    probs = jnp.where(allowed[None], jnp.exp(scores - log_sum[..., None]), 0.0)
    score_grad = (probs * (prob_grad - row_delta[..., None])).astype(jnp.bfloat16)
    return (probs.astype(jnp.bfloat16), score_grad)


def per_device(queries, key_states, value_states, attn_out, out_grad, owner_ids):
    row_count, full_width = queries.shape
    inv_root = HD ** (-0.5)
    group_heads = 2
    group_width = group_heads * HD
    seq_count = lax.axis_size("seq")
    position = lax.axis_index(("grp", "seq"))
    shard_ids = jnp.arange(seq_count, dtype=jnp.int32)
    counts = jnp.sum(
        (owner_ids[:, :, None] == shard_ids[None, None, :]).astype(jnp.int32), axis=1
    ).reshape(-1)
    edge_zeros = jnp.zeros((HOPS,), jnp.int32)
    padded = jnp.concatenate([edge_zeros, counts, edge_zeros])
    nearby = lax.dynamic_slice_in_dim(padded, position, 2 * HOPS + 1)
    own_row = jnp.arange(row_count, dtype=jnp.int32)
    own_live = live_rows(nearby[HOPS], row_count)
    current = (key_states, value_states)
    pieces = [current]
    for offset in range(HOPS):
        current = passed_along((current[0], current[1]), ("grp", "seq"), 1)
        pieces.append(current)
    keys_all = jnp.concatenate([piece[0] for piece in pieces], axis=0)
    values_all = jnp.concatenate([piece[1] for piece in pieces], axis=0)
    key_live = jnp.concatenate(
        [live_rows(nearby[HOPS - offset], row_count) for offset in range(HOPS + 1)]
    )
    window_index = jnp.arange((HOPS + 1) * row_count, dtype=jnp.int32)
    window_back = window_index // row_count
    window_row = window_index % row_count
    allowed = (
        own_live[:, None]
        & key_live[None, :]
        & ((window_back[None, :] > 0) | (window_row[None, :] <= own_row[:, None]))
    )
    query_parts = []
    key_parts = []
    value_parts = []
    sum_parts = []
    delta_parts = []
    for column in range(0, full_width, group_width):
        query_group = queries[:, column : column + group_width]
        key_group = keys_all[:, column : column + group_width]
        value_group = values_all[:, column : column + group_width]
        grad_group = out_grad[:, column : column + group_width]
        out_group = attn_out[:, column : column + group_width]
        scores = pair_products(query_group, key_group, group_heads) * inv_root
        log_sum = log_total(scores, allowed[None])
        row_delta = jnp.sum(
            (grad_group.astype(jnp.float32) * out_group.astype(jnp.float32)).reshape(
                row_count, group_heads, HD
            ),
            axis=-1,
        ).T
        prob_grad = pair_products(grad_group, value_group, group_heads)
        prob_bf, score_grad = grad_terms(scores, log_sum, allowed, prob_grad, row_delta)
        query_term = (
            jnp.einsum(
                "hij,jhd->ihd",
                score_grad,
                key_group.reshape(-1, group_heads, HD),
                preferred_element_type=jnp.float32,
            )
            * inv_root
        )
        query_parts.append(query_term.reshape(row_count, group_width).astype(jnp.bfloat16))
        sum_parts.append(log_sum)
        delta_parts.append(row_delta)
        key_term = (
            jnp.einsum(
                "hij,ihd->jhd",
                score_grad,
                query_group.reshape(row_count, group_heads, HD),
                preferred_element_type=jnp.float32,
            )
            * inv_root
        )
        value_term = jnp.einsum(
            "hij,ihd->jhd",
            prob_bf,
            grad_group.reshape(row_count, group_heads, HD),
            preferred_element_type=jnp.float32,
        )
        key_parts.append(key_term.reshape(-1, group_width))
        value_parts.append(value_term.reshape(-1, group_width))
    query_grad = jnp.concatenate(query_parts, axis=1)
    key_terms = jnp.concatenate(key_parts, axis=1)
    value_terms = jnp.concatenate(value_parts, axis=1)
    running = (key_terms[HOPS * row_count :], value_terms[HOPS * row_count :])
    for offset in range(HOPS - 1, -1, -1):
        arrived = passed_along((running[0], running[1]), ("grp", "seq"), -1)
        running = (
            arrived[0] + key_terms[offset * row_count : (offset + 1) * row_count],
            arrived[1] + value_terms[offset * row_count : (offset + 1) * row_count],
        )
    key_grad, value_grad = running
    return (query_grad, key_grad.astype(jnp.bfloat16), value_grad.astype(jnp.bfloat16))


def solution(mesh):
    placed = (
        P(("grp", "seq"), None),
        P(("grp", "seq"), None),
        P(("grp", "seq"), None),
        P(("grp", "seq"), None),
        P(("grp", "seq"), None),
        P(),
    )
    return jax.shard_map(
        per_device,
        mesh=mesh,
        in_specs=placed,
        out_specs=(P(("grp", "seq"), None), P(("grp", "seq"), None), P(("grp", "seq"), None)),
        check_vma=False,
    )
```

profile of v0, /device:TPU:7, one launch (start us, length us, event | category | flops | bytes accessed | tf_op | source)
XLA Modules:
  0.0 346.3 jit_solution(4553174577942491007)
XLA Ops:
  2.2 3.8 %collective-permute-start.3 = (bf16[256,2048]{0,1:T(8,128)(2,1)S(1)}, bf16[256,2048]{0,1:T(8,128)(2,1)}, u32[]{:S(2)}, u32[]{:S(2)}) collective-permute-start(bf16[256,2048]{0,1:T(8,128)(2,1)S(1)} %copy.195), channel_id=1, source_target_pairs={{0,1},{1,2},{2,3},{3,4},{4,5},{5,6},{6,7},{7,8},{8,9},{9,10},{10,1... | collective-permute-start | bytes 3145736 | tf_op jit(solution)/shard_map/ppermute | solution.py:14
  12.8 4.9 %collective-permute-done.3 = bf16[256,2048]{0,1:T(8,128)(2,1)} collective-permute-done((bf16[256,2048]{0,1:T(8,128)(2,1)S(1)}, bf16[256,2048]{0,1:T(8,128)(2,1)}, u32[]{:S(2)}, u32[]{:S(2)}) %collective-permute-start.3) | collective-permute-done | bytes 1048608 | tf_op jit(solution)/shard_map/ppermute | solution.py:14
  17.7 4.5 %collective-permute-start.4 = (bf16[256,2048]{0,1:T(8,128)(2,1)}, bf16[256,2048]{0,1:T(8,128)(2,1)S(1)}, u32[]{:S(2)}, u32[]{:S(2)}) collective-permute-start(bf16[256,2048]{0,1:T(8,128)(2,1)} %collective-permute-done.3), channel_id=1, source_target_pairs={{0,1},{1,2},{2,3},{3,4},{4,5},{5,6},{6,7},{7,8},{8,9},{9,10},{10,1... | collective-permute-start | bytes 3145736 | tf_op jit(solution)/shard_map/ppermute | solution.py:14
  65.0 3.6 %collective-permute-start.5 = (bf16[256,2048]{0,1:T(8,128)(2,1)S(1)}, bf16[256,2048]{0,1:T(8,128)(2,1)S(1)}, u32[]{:S(2)}, u32[]{:S(2)}) collective-permute-start(bf16[256,2048]{0,1:T(8,128)(2,1)S(1)} %collective-permute-done.4), channel_id=1, source_target_pairs={{0,1},{1,2},{2,3},{3,4},{4,5},{5,6},{6,7},{7,8},{8,9},{9,10},{10,1... | collective-permute-start | bytes 3145736 | tf_op jit(solution)/shard_map/ppermute | solution.py:14
  79.6 4.7 %collective-permute-done.5 = bf16[256,2048]{0,1:T(8,128)(2,1)S(1)} collective-permute-done((bf16[256,2048]{0,1:T(8,128)(2,1)S(1)}, bf16[256,2048]{0,1:T(8,128)(2,1)S(1)}, u32[]{:S(2)}, u32[]{:S(2)}) %collective-permute-start.5) | collective-permute-done | bytes 1048608 | tf_op jit(solution)/shard_map/ppermute | solution.py:14
  87.7 7.7 %collective-permute-done.2 = bf16[256,2048]{0,1:T(8,128)(2,1)S(1)} collective-permute-done((bf16[256,2048]{0,1:T(8,128)(2,1)S(1)}, bf16[256,2048]{0,1:T(8,128)(2,1)S(1)}, u32[]{:S(2)}, u32[]{:S(2)}) %collective-permute-start.2) | collective-permute-done | bytes 1048608 | tf_op jit(solution)/shard_map/ppermute | solution.py:14
  102.5 3.1 exponential_reduce_fusion
  106.7 2.8 exponential_reduce_fusion.1
  122.6 3.4 fusion.52
  131.8 3.4 fusion.60
  138.4 2.6 copy.275
  141.1 2.6 copy.291
  143.7 3.4 fusion.58
  155.4 3.4 fusion.56
  164.7 3.4 fusion.54
  174.1 2.6 fusion.64
  180.3 2.7 copy.289
  183.0 2.6 fusion.50
  196.7 12.1 %collective-permute-start.9 = (f32[256,2048]{1,0:T(8,128)}, f32[256,2048]{1,0:T(8,128)}, u32[]{:S(2)}, u32[]{:S(2)}) collective-permute-start(f32[256,2048]{1,0:T(8,128)} %slice.229), channel_id=1, source_target_pairs={{1,0},{2,1},{3,2},{4,3},{5,4},{6,5},{7,6},{8,7},{9,8},{10,9},{11,1... | collective-permute-start | bytes 6291464 | tf_op jit(solution)/shard_map/ppermute | solution.py:14
  229.9 7.6 %collective-permute-start.10 = (f32[256,2048]{1,0:T(8,128)S(1)}, f32[256,2048]{1,0:T(8,128)S(1)}, u32[]{:S(2)}, u32[]{:S(2)}) collective-permute-start(f32[256,2048]{1,0:T(8,128)S(1)} %slice_add_fusion.2), channel_id=1, source_target_pairs={{1,0},{2,1},{3,2},{4,3},{5,4},{6,5},{7,6},{8,7},{9,8},{10,9},{11,1... | collective-permute-start | bytes 6291464 | tf_op jit(solution)/shard_map/ppermute | solution.py:14
  237.5 15.1 %collective-permute-done.6 = f32[256,2048]{1,0:T(8,128)S(1)} collective-permute-done((f32[256,2048]{1,0:T(8,128)S(1)}, f32[256,2048]{1,0:T(8,128)S(1)}, u32[]{:S(2)}, u32[]{:S(2)}) %collective-permute-start.6) | collective-permute-done | bytes 2097184 | tf_op jit(solution)/shard_map/ppermute | solution.py:14
  254.5 4.6 %collective-permute-start.7 = (f32[256,2048]{1,0:T(8,128)S(1)}, f32[256,2048]{1,0:T(8,128)S(1)}, u32[]{:S(2)}, u32[]{:S(2)}) collective-permute-start(f32[256,2048]{1,0:T(8,128)S(1)} %slice_add_fusion.5), channel_id=1, source_target_pairs={{1,0},{2,1},{3,2},{4,3},{5,4},{6,5},{7,6},{8,7},{9,8},{10,9},{11,1... | collective-permute-start | bytes 6291464 | tf_op jit(solution)/shard_map/ppermute | solution.py:14
  262.8 12.3 %collective-permute-done.10 = f32[256,2048]{1,0:T(8,128)S(1)} collective-permute-done((f32[256,2048]{1,0:T(8,128)S(1)}, f32[256,2048]{1,0:T(8,128)S(1)}, u32[]{:S(2)}, u32[]{:S(2)}) %collective-permute-start.10) | collective-permute-done | bytes 2097184 | tf_op jit(solution)/shard_map/ppermute | solution.py:14
  275.1 3.3 slice_add_fusion.1
  278.4 4.6 %collective-permute-start.11 = (f32[256,2048]{1,0:T(8,128)}, f32[256,2048]{1,0:T(8,128)}, u32[]{:S(2)}, u32[]{:S(2)}) collective-permute-start(f32[256,2048]{1,0:T(8,128)} %slice_add_fusion.1), channel_id=1, source_target_pairs={{1,0},{2,1},{3,2},{4,3},{5,4},{6,5},{7,6},{8,7},{9,8},{10,9},{11,1... | collective-permute-start | bytes 6291464 | tf_op jit(solution)/shard_map/ppermute | solution.py:14
  282.9 14.6 %collective-permute-done.7 = f32[256,2048]{1,0:T(8,128)S(1)} collective-permute-done((f32[256,2048]{1,0:T(8,128)S(1)}, f32[256,2048]{1,0:T(8,128)S(1)}, u32[]{:S(2)}, u32[]{:S(2)}) %collective-permute-start.7) | collective-permute-done | bytes 2097184 | tf_op jit(solution)/shard_map/ppermute | solution.py:14
  297.6 3.2 slice_add_fusion.4
  300.8 4.6 %collective-permute-start.8 = (f32[256,2048]{1,0:T(8,128)}, f32[256,2048]{1,0:T(8,128)}, u32[]{:S(2)}, u32[]{:S(2)}) collective-permute-start(f32[256,2048]{1,0:T(8,128)} %slice_add_fusion.4), channel_id=1, source_target_pairs={{1,0},{2,1},{3,2},{4,3},{5,4},{6,5},{7,6},{8,7},{9,8},{10,9},{11,1... | collective-permute-start | bytes 6291464 | tf_op jit(solution)/shard_map/ppermute | solution.py:14
  314.4 5.8 %collective-permute-done.11 = f32[256,2048]{1,0:T(8,128)} collective-permute-done((f32[256,2048]{1,0:T(8,128)}, f32[256,2048]{1,0:T(8,128)}, u32[]{:S(2)}, u32[]{:S(2)}) %collective-permute-start.11) | collective-permute-done | bytes 2097184 | tf_op jit(solution)/shard_map/ppermute | solution.py:14
  320.1 3.5 fusion
  323.6 19.0 %collective-permute-done.8 = f32[256,2048]{1,0:T(8,128)} collective-permute-done((f32[256,2048]{1,0:T(8,128)}, f32[256,2048]{1,0:T(8,128)}, u32[]{:S(2)}, u32[]{:S(2)}) %collective-permute-start.8) | collective-permute-done | bytes 2097184 | tf_op jit(solution)/shard_map/ppermute | solution.py:14
  342.6 3.5 fusion.1
  (364 shorter events, 165.1 us)
Async XLA Ops:
  2.2 15.5 %collective-permute-start.3 = (bf16[256,2048]{0,1:T(8,128)(2,1)S(1)}, bf16[256,2048]{0,1:T(8,128)(2,1)}, u32[]{:S(2)}, u32[]{:S(2)}) collective-permute-start(bf16[256,2048]{0,1:T(8,128)(2,1)S(1)} %copy.195), channel_id=1, source_target_pairs={{0,1},{1,2},{2,3},{3,4},{4,5},{5,6},{6,7},{7,8},{8,9},{9,10},{10,1... | collective-permute-start | bytes 3145736 | tf_op jit(solution)/shard_map/ppermute | solution.py:14
  6.6 52.6 %collective-permute-start = (bf16[256,2048]{0,1:T(8,128)(2,1)S(1)}, bf16[256,2048]{0,1:T(8,128)(2,1)}, u32[]{:S(2)}, u32[]{:S(2)}) collective-permute-start(bf16[256,2048]{0,1:T(8,128)(2,1)S(1)} %copy.190), channel_id=1, source_target_pairs={{0,1},{1,2},{2,3},{3,4},{4,5},{5,6},{6,7},{7,8},{8,9},{9,10},{10,1... | collective-permute-start | bytes 3145736 | tf_op jit(solution)/shard_map/ppermute | solution.py:14
  10.9 11.4 %copy-start.106 = (s32[4,16]{1,0:T(4,128)S(1)}, s32[4,16]{1,0:T(4,128)}, u32[]{:S(2)}) copy-start(s32[4,16]{1,0:T(4,128)} %param.11) | copy-start | bytes 772
  17.7 47.3 %collective-permute-start.4 = (bf16[256,2048]{0,1:T(8,128)(2,1)}, bf16[256,2048]{0,1:T(8,128)(2,1)S(1)}, u32[]{:S(2)}, u32[]{:S(2)}) collective-permute-start(bf16[256,2048]{0,1:T(8,128)(2,1)} %collective-permute-done.3), channel_id=1, source_target_pairs={{0,1},{1,2},{2,3},{3,4},{4,5},{5,6},{6,7},{7,8},{8,9},{9,10},{10,1... | collective-permute-start | bytes 3145736 | tf_op jit(solution)/shard_map/ppermute | solution.py:14
  44.8 11.8 %copy-start.82 = (bf16[256,256]{1,0:T(8,128)(2,1)S(1)}, bf16[256,256]{1,0:T(8,128)(2,1)}, u32[]{:S(2)}) copy-start(bf16[256,256]{1,0:T(8,128)(2,1)} %get-tuple-element.50) | copy-start | bytes 393220
  46.6 32.1 %copy-start.83 = (bf16[256,256]{0,1:T(8,128)(2,1)}, bf16[256,256]{0,1:T(8,128)(2,1)S(1)}, u32[]{:S(2)}) copy-start(bf16[256,256]{0,1:T(8,128)(2,1)S(1)} %copy.375) | copy-start | bytes 393220
  59.1 17.1 %collective-permute-start.1 = (bf16[256,2048]{0,1:T(8,128)(2,1)}, bf16[256,2048]{0,1:T(8,128)(2,1)S(1)}, u32[]{:S(2)}, u32[]{:S(2)}) collective-permute-start(bf16[256,2048]{0,1:T(8,128)(2,1)} %collective-permute-done), channel_id=1, source_target_pairs={{0,1},{1,2},{2,3},{3,4},{4,5},{5,6},{6,7},{7,8},{8,9},{9,10},{10,1... | collective-permute-start | bytes 3145736 | tf_op jit(solution)/shard_map/ppermute | solution.py:14
  65.0 19.2 %collective-permute-start.5 = (bf16[256,2048]{0,1:T(8,128)(2,1)S(1)}, bf16[256,2048]{0,1:T(8,128)(2,1)S(1)}, u32[]{:S(2)}, u32[]{:S(2)}) collective-permute-start(bf16[256,2048]{0,1:T(8,128)(2,1)S(1)} %collective-permute-done.4), channel_id=1, source_target_pairs={{0,1},{1,2},{2,3},{3,4},{4,5},{5,6},{6,7},{7,8},{8,9},{9,10},{10,1... | collective-permute-start | bytes 3145736 | tf_op jit(solution)/shard_map/ppermute | solution.py:14
  76.2 19.2 %collective-permute-start.2 = (bf16[256,2048]{0,1:T(8,128)(2,1)S(1)}, bf16[256,2048]{0,1:T(8,128)(2,1)S(1)}, u32[]{:S(2)}, u32[]{:S(2)}) collective-permute-start(bf16[256,2048]{0,1:T(8,128)(2,1)S(1)} %collective-permute-done.1), channel_id=1, source_target_pairs={{0,1},{1,2},{2,3},{3,4},{4,5},{5,6},{6,7},{7,8},{8,9},{9,10},{10,1... | collective-permute-start | bytes 3145736 | tf_op jit(solution)/shard_map/ppermute | solution.py:14
  98.5 8.2 %copy-start.9 = (f32[2,1024,256]{2,1,0:T(8,128)}, f32[2,1024,256]{2,1,0:T(8,128)S(1)}, u32[]{:S(2)}) copy-start(f32[2,1024,256]{2,1,0:T(8,128)S(1)} %fusion.135) | copy-start | bytes 6291460
  99.3 7.4 %copy-start.1 = (f32[2,1024,256]{2,1,0:T(8,128)}, f32[2,1024,256]{2,1,0:T(8,128)S(1)}, u32[]{:S(2)}) copy-start(f32[2,1024,256]{2,1,0:T(8,128)S(1)} %fusion.134) | copy-start | bytes 6291460
  99.8 6.9 %copy-start.3 = (f32[2,1024,256]{2,1,0:T(8,128)}, f32[2,1024,256]{2,1,0:T(8,128)S(1)}, u32[]{:S(2)}) copy-start(f32[2,1024,256]{2,1,0:T(8,128)S(1)} %fusion.133) | copy-start | bytes 6291460
  100.4 6.3 %copy-start.5 = (f32[2,1024,256]{2,1,0:T(8,128)}, f32[2,1024,256]{2,1,0:T(8,128)S(1)}, u32[]{:S(2)}) copy-start(f32[2,1024,256]{2,1,0:T(8,128)S(1)} %fusion.132) | copy-start | bytes 6291460
  195.2 18.2 %copy-start = (f32[1024,2048]{1,0:T(8,128)}, f32[1024,2048]{1,0:T(8,128)S(1)}, u32[]{:S(2)}) copy-start(f32[1024,2048]{1,0:T(8,128)S(1)} %constant_dynamic-update-slice_fusion.16) | copy-start | bytes 25165828
  195.2 13.6 %copy-start.33 = (f32[1024,256]{1,0:T(8,128)S(1)}, f32[1024,256]{1,0:T(8,128)}, u32[]{:S(2)}) copy-start(f32[1024,256]{1,0:T(8,128)} %copy.273) | copy-start | bytes 3145732
  196.7 13.3 %copy-start.21 = (f32[1024,256]{1,0:T(8,128)S(1)}, f32[1024,256]{1,0:T(8,128)}, u32[]{:S(2)}) copy-start(f32[1024,256]{1,0:T(8,128)} %copy.274) | copy-start | bytes 3145732
  196.7 14.4 %copy-start.23 = (f32[1024,256]{1,0:T(8,128)S(1)}, f32[1024,256]{1,0:T(8,128)}, u32[]{:S(2)}) copy-start(f32[1024,256]{1,0:T(8,128)} %copy.275) | copy-start | bytes 3145732
  196.7 30.7 %collective-permute-start.9 = (f32[256,2048]{1,0:T(8,128)}, f32[256,2048]{1,0:T(8,128)}, u32[]{:S(2)}, u32[]{:S(2)}) collective-permute-start(f32[256,2048]{1,0:T(8,128)} %slice.229), channel_id=1, source_target_pairs={{1,0},{2,1},{3,2},{4,3},{5,4},{6,5},{7,6},{8,7},{9,8},{10,9},{11,1... | collective-permute-start | bytes 6291464 | tf_op jit(solution)/shard_map/ppermute | solution.py:14
  225.3 27.4 %collective-permute-start.6 = (f32[256,2048]{1,0:T(8,128)S(1)}, f32[256,2048]{1,0:T(8,128)S(1)}, u32[]{:S(2)}, u32[]{:S(2)}) collective-permute-start(f32[256,2048]{1,0:T(8,128)S(1)} %slice.225), channel_id=1, source_target_pairs={{1,0},{2,1},{3,2},{4,3},{5,4},{6,5},{7,6},{8,7},{9,8},{10,9},{11,1... | collective-permute-start | bytes 6291464 | tf_op jit(solution)/shard_map/ppermute | solution.py:14
  229.8 29.3 %copy-start.39 = (bf16[2,256,1024]{1,2,0:T(8,128)(2,1)S(1)}, bf16[2,256,1024]{1,2,0:T(8,128)(2,1)}, u32[]{:S(2)}) copy-start(bf16[2,256,1024]{1,2,0:T(8,128)(2,1)} %copy-done.38) | copy-start | bytes 3145732
  229.8 29.3 %copy-start.55 = (bf16[1024,256]{0,1:T(8,128)(2,1)S(1)}, bf16[1024,256]{0,1:T(8,128)(2,1)}, u32[]{:S(2)}) copy-start(bf16[1024,256]{0,1:T(8,128)(2,1)} %copy-done.54) | copy-start | bytes 1572868
  229.9 29.6 %copy-start.20 = (bf16[1024,256]{0,1:T(8,128)(2,1)S(1)}, bf16[1024,256]{0,1:T(8,128)(2,1)}, u32[]{:S(2)}) copy-start(bf16[1024,256]{0,1:T(8,128)(2,1)} %copy-done.19) | copy-start | bytes 1572868
  229.9 29.6 %copy-start.41 = (bf16[2,256,1024]{1,2,0:T(8,128)(2,1)S(1)}, bf16[2,256,1024]{1,2,0:T(8,128)(2,1)}, u32[]{:S(2)}) copy-start(bf16[2,256,1024]{1,2,0:T(8,128)(2,1)} %copy-done.40) | copy-start | bytes 3145732
  229.9 45.2 %collective-permute-start.10 = (f32[256,2048]{1,0:T(8,128)S(1)}, f32[256,2048]{1,0:T(8,128)S(1)}, u32[]{:S(2)}, u32[]{:S(2)}) collective-permute-start(f32[256,2048]{1,0:T(8,128)S(1)} %slice_add_fusion.2), channel_id=1, source_target_pairs={{1,0},{2,1},{3,2},{4,3},{5,4},{6,5},{7,6},{8,7},{9,8},{10,9},{11,1... | collective-permute-start | bytes 6291464 | tf_op jit(solution)/shard_map/ppermute | solution.py:14
  254.5 43.0 %collective-permute-start.7 = (f32[256,2048]{1,0:T(8,128)S(1)}, f32[256,2048]{1,0:T(8,128)S(1)}, u32[]{:S(2)}, u32[]{:S(2)}) collective-permute-start(f32[256,2048]{1,0:T(8,128)S(1)} %slice_add_fusion.5), channel_id=1, source_target_pairs={{1,0},{2,1},{3,2},{4,3},{5,4},{6,5},{7,6},{8,7},{9,8},{10,9},{11,1... | collective-permute-start | bytes 6291464 | tf_op jit(solution)/shard_map/ppermute | solution.py:14
  278.4 27.0 %copy-start.12 = (bf16[1024,256]{0,1:T(8,128)(2,1)S(1)}, bf16[1024,256]{0,1:T(8,128)(2,1)}, u32[]{:S(2)}) copy-start(bf16[1024,256]{0,1:T(8,128)(2,1)} %copy-done.11) | copy-start | bytes 1572868
  278.4 27.0 %copy-start.47 = (bf16[2,256,1024]{1,2,0:T(8,128)(2,1)S(1)}, bf16[2,256,1024]{1,2,0:T(8,128)(2,1)}, u32[]{:S(2)}) copy-start(bf16[2,256,1024]{1,2,0:T(8,128)(2,1)} %copy-done.46) | copy-start | bytes 3145732
  278.4 41.8 %collective-permute-start.11 = (f32[256,2048]{1,0:T(8,128)}, f32[256,2048]{1,0:T(8,128)}, u32[]{:S(2)}, u32[]{:S(2)}) collective-permute-start(f32[256,2048]{1,0:T(8,128)} %slice_add_fusion.1), channel_id=1, source_target_pairs={{1,0},{2,1},{3,2},{4,3},{5,4},{6,5},{7,6},{8,7},{9,8},{10,9},{11,1... | collective-permute-start | bytes 6291464 | tf_op jit(solution)/shard_map/ppermute | solution.py:14
  300.8 10.9 %copy-start.45 = (bf16[2,256,1024]{1,2,0:T(8,128)(2,1)S(1)}, bf16[2,256,1024]{1,2,0:T(8,128)(2,1)}, u32[]{:S(2)}) copy-start(bf16[2,256,1024]{1,2,0:T(8,128)(2,1)} %copy-done.44) | copy-start | bytes 3145732
  300.8 41.8 %collective-permute-start.8 = (f32[256,2048]{1,0:T(8,128)}, f32[256,2048]{1,0:T(8,128)}, u32[]{:S(2)}, u32[]{:S(2)}) collective-permute-start(f32[256,2048]{1,0:T(8,128)} %slice_add_fusion.4), channel_id=1, source_target_pairs={{1,0},{2,1},{3,2},{4,3},{5,4},{6,5},{7,6},{8,7},{9,8},{10,9},{11,1... | collective-permute-start | bytes 6291464 | tf_op jit(solution)/shard_map/ppermute | solution.py:14
  306.4 7.3 %copy-start.51 = (bf16[2,256,1024]{1,2,0:T(8,128)(2,1)S(1)}, bf16[2,256,1024]{1,2,0:T(8,128)(2,1)}, u32[]{:S(2)}) copy-start(bf16[2,256,1024]{1,2,0:T(8,128)(2,1)} %copy-done.50) | copy-start | bytes 3145732
  314.3 9.3 %copy-start.95 = (bf16[256,2048]{1,0:T(8,128)(2,1)}, bf16[256,2048]{1,0:T(8,128)(2,1)S(1)}, u32[]{:S(2)}) copy-start(bf16[256,2048]{1,0:T(8,128)(2,1)S(1)} %constant_dynamic-update-slice_fusion) | copy-start | bytes 3145732
  (87 other events, 221.7 us)
where the time goes:
time: 353 us; the launch traced here: 346 us
  local copies, waits for them, and re-layouts  112 us (32%)
  waiting for transfers between devices  84.2 us (24%)
  starting transfers between devices  53.7 us (15%)
  matrix products  53 us (15%)
  other arithmetic  41.5 us (12%)
    ppermute x12, waiting for transfers between devices, passed_along(): return lax.ppermute(array, axis, pairs)  84.2 us
    unnamed x261, local copies, waits for them, and re-layouts  60.7 us
    ppermute x12, starting transfers between devices, passed_along(): return lax.ppermute(array, axis, pairs)  53.7 us
    dot_general x8, matrix products, per_device(): jnp.einsum('hij,ihd->jhd', prob_bf, grad_group.reshape(row_count, group_h...  23.9 us
    reshape x8, local copies, waits for them, and re-layouts, per_device(): value_parts.append(value_term.reshape(-1, group_width))  19.3 us
    reshape x8, local copies, waits for them, and re-layouts, per_device(): key_parts.append(key_term.reshape(-1, group_width))  13.4 us
    dot_general x16, matrix products, pair_products(): jnp.einsum('ihd,jhd->hij', first_op.reshape(first_op.shape[0], head_count...  13.3 us
    dot_general x8, matrix products, per_device(): jnp.einsum('hij,ihd->jhd', score_grad, query_group.reshape(row_count, gro...  10.6 us
  transfers between devices with their start and end apart: 12, of which 8 were waited for; matrix products, arithmetic and copies ran while one was open for 29% of the time, Pallas kernels for 0%

commit v1 on v0

v1 whole, which is shorter than its diff:
```python
import functools
import math

import jax
import jax.numpy as jnp
from jax import lax
from jax.experimental import pallas as pl
from jax.experimental.pallas import tpu as pltpu
from jax.sharding import PartitionSpec as P

HD = 128
BLK = 128
SL = 256
MESH = pl.DeviceIdType.MESH
F32 = jnp.float32
BF16 = jnp.bfloat16
NEG = -1e30
KEY, VAL, QRY, GRD, OUT = range(5)


def dot(a, b, dims):
    return lax.dot_general(a, b, (dims, ((), ())), preferred_element_type=F32)


def kernel(w, nh, owners, q_in, k_in, v_in, o_in, g_in, dq_out, dk_out, dv_out,
           own, kv_out, kv_in, back_out, back_in, part_far, part_own, stage,
           s_buf, dp_buf, p_buf, ds_buf,
           loc_sem, xs_sem, xr_sem, as_sem, ar_sem, bs_sem, br_sem,
           ras_sem, rar_sem, rbs_sem, rbr_sem, ol_sem, os_sem, or_sem):
    n_seq = lax.axis_size("seq")
    n_all = lax.axis_size("grp") * n_seq
    me = lax.axis_index("grp") * n_seq + lax.axis_index("seq")
    core = lax.rem(me, 2)
    even = me - core
    na = w - 2

    def dev(d):
        d = lax.rem(d + n_all, n_all)
        return (d // n_seq, lax.rem(d, n_seq))

    mate = dev(even + 1 - core)
    ahead = dev(me + 2)
    behind = dev(me - 2)

    barrier = pltpu.get_barrier_semaphore()
    for other in (mate, ahead, behind):
        pl.semaphore_signal(barrier, inc=1, device_id=other, device_id_type=MESH)

    inputs = (k_in, v_in, q_in, g_in, o_in)
    outputs = (dq_out, dk_out, dv_out)

    def cols(which_core, h):
        return pl.ds(pl.multiple_of((which_core * nh + h) * HD, HD), HD)

    mine = pl.ds(pl.multiple_of(core * SL, SL), SL)
    mates = pl.ds(pl.multiple_of((1 - core) * SL, SL), SL)

    def local_in(h, a):
        return pltpu.make_async_copy(inputs[a].at[:, cols(core, h)], own.at[h, a, mine], loc_sem.at[h, a])

    def mate_in(h, a):
        return pltpu.make_async_remote_copy(
            src_ref=inputs[a].at[:, cols(1 - core, h)], dst_ref=own.at[h, a, mine],
            send_sem=xs_sem.at[h, a], recv_sem=xr_sem.at[h, a], device_id=mate, device_id_type=MESH)

    def mate_in_arrival(h, a):
        return pltpu.make_async_remote_copy(
            src_ref=own.at[h, a, mates], dst_ref=own.at[h, a, mates],
            send_sem=xs_sem.at[h, a], recv_sem=xr_sem.at[h, a], device_id=mate, device_id_type=MESH)

    def hop(src, dst, h, lo, size, ss, rs, to):
        return pltpu.make_async_remote_copy(
            src_ref=src.at[h, pl.ds(lo, size)], dst_ref=dst.at[h, pl.ds(lo, size)],
            send_sem=ss.at[h], recv_sem=rs.at[h], device_id=to, device_id_type=MESH)

    def send_a(h):
        return hop(kv_out, kv_in, h, 0, na, as_sem, ar_sem, ahead)

    def send_b(h):
        return hop(kv_out, kv_in, h, na, 2, bs_sem, br_sem, ahead)

    def back_a(h):
        return hop(back_out, back_in, h, 0, na, ras_sem, rar_sem, behind)

    def back_b(h):
        return hop(back_out, back_in, h, na, 2, rbs_sem, rbr_sem, behind)

    def local_res(h, a):
        return pltpu.make_async_copy(stage.at[h, a, mine], outputs[a].at[:, cols(core, h)], ol_sem.at[h, a])

    def mate_res(h, a):
        return pltpu.make_async_remote_copy(
            src_ref=stage.at[h, a, mates], dst_ref=outputs[a].at[:, cols(core, h)],
            send_sem=os_sem.at[h, a], recv_sem=or_sem.at[h, a], device_id=mate, device_id_type=MESH)

    def mate_res_arrival(h, a):
        return pltpu.make_async_remote_copy(
            src_ref=stage.at[h, a, mates], dst_ref=outputs[a].at[:, cols(1 - core, h)],
            send_sem=os_sem.at[h, a], recv_sem=or_sem.at[h, a], device_id=mate, device_id_type=MESH)

    def live_count(shard):
        s = jnp.maximum(shard, 0)
        total = jnp.int32(0)
        for b in range(owners.shape[1]):
            total += (owners[s // n_seq, b] == lax.rem(s, n_seq)).astype(jnp.int32)
        return jnp.where(shard >= 0, total, 0)

    c_m3, c_m2, c_m1, c_e, c_o = [live_count(even + i) for i in (-3, -2, -1, 0, 1)]
    own_live = (c_e >= 1, c_e >= 2, c_o >= 1, c_o >= 2)

    def arrived_kind(t):
        passed = jnp.bool_(False)
        if t == w - 1:
            passed = c_m3 >= 1
        elif t == w - 2:
            passed = c_m3 >= 2
        own_there = c_m1 + c_m2 > t
        return passed, own_there

    near_ok = []
    far_ok = []
    for t in range(w):
        passed, own_there = arrived_kind(t)
        near_ok.append(jnp.logical_or(passed, own_there))
        far_ok.append(jnp.logical_and(jnp.logical_not(passed), own_there))

    def fetch(h, a_list):
        for a in a_list:
            local_in(h, a).start()
            mate_in(h, a).start()

    def fetched(h, a_list):
        for a in a_list:
            local_in(h, a).wait()
            mate_in_arrival(h, a).wait_recv()

    def own_block(h, a, slot):
        return own[h, a, slot * BLK:(slot + 1) * BLK, :]

    def own_pick(h, x, t):
        e0, e1, o0, o1 = 0, 1, 2, 3
        if t == 0:
            return jnp.where(c_o >= 1, own_block(h, x, o0), own_block(h, x, e0))
        if t == 1:
            return jnp.where(c_o >= 2, own_block(h, x, o1),
                             jnp.where(c_o >= 1, own_block(h, x, e0), own_block(h, x, e1)))
        if t == 2:
            return jnp.where(c_o >= 2, own_block(h, x, e0), own_block(h, x, e1))
        return own_block(h, x, e1)

    def make_a(h):
        for t in range(na):
            for x in (KEY, VAL):
                kv_out[h, t, x] = own_pick(h, x, t)

    def make_b(h):
        for x in (KEY, VAL):
            first, second = kv_in[h, 0, x], kv_in[h, 1, x]
            if w - 2 < 4:
                second = jnp.where(c_m1 >= 2, second, own_pick(h, x, w - 2))
            if w - 1 < 4:
                first = jnp.where(c_m1 >= 1, first, own_pick(h, x, w - 1))
            kv_out[h, w - 2, x] = second
            kv_out[h, w - 1, x] = first

    inv_root = HD ** (-0.5)
    exp_scale = inv_root * math.log2(math.e)
    row_id = lax.broadcasted_iota(jnp.int32, (BLK, SL), 0)
    col_id = lax.broadcasted_iota(jnp.int32, (BLK, SL), 1)
    first_half = lax.broadcasted_iota(jnp.int32, (1, SL), 1) < BLK

    def compute(h):
        keys, vals = own[h, KEY], own[h, VAL]
        far_keys = kv_in[h, :, KEY].reshape(w * BLK, HD)
        far_vals = kv_in[h, :, VAL].reshape(w * BLK, HD)
        prod = own[h, GRD].astype(F32) * own[h, OUT].astype(F32)
        delta_all = jnp.sum(prod.T, axis=0, keepdims=True)
        for a in range(2):
            nk = SL * (a + 1)
            rows = slice(a * SL, (a + 1) * SL)
            query, grad = own[h, QRY, rows], own[h, GRD, rows]
            delta = delta_all[:, rows]
            s_buf[0:nk] = dot(keys[:nk], query, ((1,), (1,)))
            s_buf[2 * SL:] = dot(far_keys, query, ((1,), (1,)))
            dp_buf[0:nk] = dot(vals[:nk], grad, ((1,), (1,)))
            dp_buf[2 * SL:] = dot(far_vals, grad, ((1,), (1,)))
            blocks = list(range(nk // BLK)) + [4 + t for t in range(w)]
            top = None
            for b in blocks:
                at = slice(b * BLK, (b + 1) * BLK)
                if b >= 4:
                    ok = (near_ok, far_ok)[a][b - 4]
                else:
                    ok = own_live[b]
                x = s_buf[at] + jnp.where(ok, 0.0, NEG).astype(F32)
                if b < 4 and b >= 2 * a:
                    x = jnp.where(row_id + (b - 2 * a) * BLK <= col_id, x, NEG)
                s_buf[at] = x
                high = jnp.max(x, axis=0, keepdims=True)
                top = high if top is None else jnp.maximum(top, high)
            total = None
            for b in blocks:
                at = slice(b * BLK, (b + 1) * BLK)
                e = jnp.exp2((s_buf[at] - top) * exp_scale)
                s_buf[at] = e
                part = jnp.sum(e, axis=0, keepdims=True)
                total = part if total is None else total + part
            live = jnp.where(first_half, jnp.where(own_live[2 * a], 1.0, 0.0).astype(F32),
                             jnp.where(own_live[2 * a + 1], 1.0, 0.0).astype(F32))
            scale = live / total
            for b in blocks:
                at = slice(b * BLK, (b + 1) * BLK)
                prob = s_buf[at] * scale
                p_buf[at, rows] = prob.astype(BF16)
                ds_buf[at, rows] = (prob * (dp_buf[at] - delta)).astype(BF16)
            dq = dot(ds_buf[0:nk, rows], keys[:nk], ((0,), (0,)))
            dq += dot(ds_buf[2 * SL:, rows], far_keys, ((0,), (0,)))
            stage[h, 0, rows] = (dq * inv_root).astype(BF16)
        second = slice(SL, 2 * SL)
        query, grad = own[h, QRY], own[h, GRD]
        nat = ((1,), (0,))
        part_own[h, 0, 0:SL] = dot(ds_buf[0:SL], query, nat) * inv_root
        part_own[h, 0, second] = dot(ds_buf[second, second], query[second], nat) * inv_root
        part_own[h, 1, 0:SL] = dot(p_buf[0:SL], grad, nat)
        part_own[h, 1, second] = dot(p_buf[second, second], grad[second], nat)
        far = slice(2 * SL, (4 + na) * BLK)
        part_far[h, :, 0] = (dot(ds_buf[far], query, nat) * inv_root).reshape(na, BLK, HD)
        part_far[h, :, 1] = dot(p_buf[far], grad, nat).reshape(na, BLK, HD)
        far = slice((4 + na) * BLK, (4 + w) * BLK)
        back_out[h, na:w, 0] = (dot(ds_buf[far], query, nat) * inv_root).astype(BF16).reshape(2, BLK, HD)
        back_out[h, na:w, 1] = dot(p_buf[far], grad, nat).astype(BF16).reshape(2, BLK, HD)

    def back_sums(h):
        for x in range(2):
            for t in range(na):
                term = part_far[h, t, x]
                if t == 0:
                    term += jnp.where(c_m1 >= 1, back_in[h, w - 1, x].astype(F32), 0.0)
                if t == 1:
                    term += jnp.where(c_m1 >= 2, back_in[h, w - 2, x].astype(F32), 0.0)
                back_out[h, t, x] = term.astype(BF16)

    def finish(h):
        for x in range(2):
            got = [back_in[h, t, x].astype(F32) for t in range(4)]
            adds = (
                jnp.where(c_e >= 1, jnp.where(c_o >= 2, got[2], jnp.where(c_o >= 1, got[1], got[0])), 0.0),
                jnp.where(c_e >= 2, jnp.where(c_o >= 2, got[3], jnp.where(c_o >= 1, got[2], got[1])), 0.0),
                jnp.where(c_o >= 1, got[0], 0.0),
                jnp.where(c_o >= 2, got[1], 0.0),
            )
            for b in range(4):
                at = slice(b * BLK, (b + 1) * BLK)
                stage[h, 1 + x, at] = (part_own[h, x, at] + adds[b]).astype(BF16)

    pl.semaphore_wait(barrier, 3)
    early = min(2, nh)
    for h in range(early):
        fetch(h, (KEY, VAL))
    for h in range(early):
        fetched(h, (KEY, VAL))
        make_a(h)
        send_a(h).start()
    for h in range(early):
        fetch(h, (QRY, GRD, OUT))

    @pl.loop(early, nh)
    def _(h):
        fetch(h, (KEY, VAL, QRY, GRD, OUT))

    @pl.loop(0, nh + 3)
    def _(step):
        @pl.when(step < nh)
        def _():
            h = step
            send_a(h).wait_recv()
            make_b(h)
            send_b(h).start()

        @pl.when(step + early < nh)
        def _():
            h = step + early
            fetched(h, (KEY, VAL))
            make_a(h)
            send_a(h).start()

        @pl.when(jnp.logical_and(step >= 1, step <= nh))
        def _():
            h = step - 1
            fetched(h, (QRY, GRD, OUT))
            send_b(h).wait_recv()
            compute(h)
            back_b(h).start()
            local_res(h, 0).start()
            mate_res(h, 0).start()

        @pl.when(jnp.logical_and(step >= 2, step <= nh + 1))
        def _():
            h = step - 2
            back_b(h).wait_recv()
            back_sums(h)
            back_a(h).start()

        @pl.when(step >= 3)
        def _():
            h = step - 3
            back_a(h).wait_recv()
            finish(h)
            for a in (1, 2):
                local_res(h, a).start()
                mate_res(h, a).start()

    @pl.loop(0, nh)
    def _(h):
        for a in range(5):
            mate_in(h, a).wait_send()
        send_a(h).wait_send()
        send_b(h).wait_send()
        back_a(h).wait_send()
        back_b(h).wait_send()
        for a in range(3):
            local_res(h, a).wait()
            mate_res(h, a).wait_send()
            mate_res_arrival(h, a).wait_recv()


def fused(w, owners, queries, key_states, value_states, attn_out, out_grad):
    width = queries.shape[1]
    nh = width // (2 * HD)
    anywhere = pl.BlockSpec(memory_space=pl.ANY)
    dma = pltpu.SemaphoreType.DMA
    slots = pltpu.VMEM((nh, w, 2, BLK, HD), BF16)
    return pl.pallas_call(
        functools.partial(kernel, w, nh),
        out_shape=[jax.ShapeDtypeStruct(queries.shape, BF16)] * 3,
        in_specs=[pl.BlockSpec(memory_space=pltpu.SMEM)] + [anywhere] * 5,
        out_specs=[anywhere] * 3,
        scratch_shapes=[
            pltpu.VMEM((nh, 5, 2 * SL, HD), BF16),
            slots, slots, slots, slots,
            pltpu.VMEM((nh, w - 2, 2, BLK, HD), F32),
            pltpu.VMEM((nh, 2, 2 * SL, HD), F32),
            pltpu.VMEM((nh, 3, 2 * SL, HD), BF16),
            pltpu.VMEM(((4 + w) * BLK, SL), F32),
            pltpu.VMEM(((4 + w) * BLK, SL), F32),
            pltpu.VMEM(((4 + w) * BLK, 2 * SL), BF16),
            pltpu.VMEM(((4 + w) * BLK, 2 * SL), BF16),
            dma((nh, 5)), dma((nh, 5)), dma((nh, 5)),
            dma((nh,)), dma((nh,)), dma((nh,)), dma((nh,)),
            dma((nh,)), dma((nh,)), dma((nh,)), dma((nh,)),
            dma((nh, 3)), dma((nh, 3)), dma((nh, 3)),
        ],
        compiler_params=pltpu.CompilerParams(
            collective_id=w - 4, has_side_effects=True, vmem_limit_bytes=56 * 2**20),
        name="slots%d" % w,
    )(owners, queries, key_states, value_states, attn_out, out_grad)


def per_device(queries, key_states, value_states, attn_out, out_grad, owner_ids):
    n_grp, n_seq = lax.axis_size("grp"), lax.axis_size("seq")
    shard = (owner_ids + n_seq * jnp.arange(n_grp, dtype=jnp.int32)[:, None]).reshape(1, -1)
    first = 2 * jnp.arange(n_grp * n_seq // 2 - 1, dtype=jnp.int32)[:, None] - 1
    inside = jnp.logical_and(shard >= first, shard <= first + 2)
    widest = jnp.max(jnp.sum(inside.astype(jnp.int32), axis=1))
    return lax.switch(
        jnp.clip(widest - 4, 0, 2),
        [functools.partial(fused, w) for w in (4, 5, 6)],
        owner_ids, queries, key_states, value_states, attn_out, out_grad)


def solution(mesh):
    rows = P(("grp", "seq"), None)
    return jax.shard_map(
        per_device,
        mesh=mesh,
        in_specs=(rows,) * 5 + (P(),),
        out_specs=(rows,) * 3,
        check_vma=False,
    )
```

time: 353 us -> 84 us (0.24)
  the two profiles are of different devices: /device:TPU:7 before, /device:TPU:1 now
where the time goes in v1:
time: 84 us; the launch traced here: 83.8 us
  Pallas kernels  77.9 us (93%)
  local copies, waits for them, and re-layouts  3.67 us (4%)
  between operations  1.32 us (2%)
  other arithmetic  0.9 us (1%)
    pallas_call x1, Pallas kernels, fused(): pl.pallas_call(functools.partial(kernel, w, nh), out_shape=[jax.ShapeDtyp...  77.9 us
    unnamed x5, local copies, waits for them, and re-layouts  3.59 us

profile of v1, /device:TPU:1, one launch (start us, length us, event | category | flops | bytes accessed | tf_op | source)
XLA Modules:
  0.0 83.8 jit_solution(14747503977977202370)
XLA Ops:
  0.7 0.0 copy-start
  0.7 0.7 copy-done
  1.3 0.1 broadcast_add_fusion
  1.4 0.1 ge.15
  1.5 0.2 convert_reduce_fusion
  1.7 0.6 reduce_max.9
  3.0 77.9 %conditional.1 = ((bf16[256,2048]{1,0:T(8,128)(2,1)S(1)}, bf16[256,2048]{1,0:T(8,128)(2,1)S(1)}, bf16[256,2048]{1,0:T(8,128)(2,1)S(1)})) conditional(s32[]{:T(128)} %clamp.3, (s32[4,16]{1,0:T(4,128)S(1)}, bf16[256,2048]{1,0:T(8,128)(2,1)}, bf16[256,2048]{1,0:T(8,128)(2,1)}, bf16[256,2048]{1,0:T(8,128)(2,1)}, ...), branch_computations={%region_2.3_spmd, %region_3.4_spmd, %region_4.5_spmd} | conditional | bytes 8 | solution.py:365
  3.0 77.9 %slots4.1 = (bf16[256,2048]{1,0:T(8,128)(2,1)S(1)}, bf16[256,2048]{1,0:T(8,128)(2,1)S(1)}, bf16[256,2048]{1,0:T(8,128)(2,1)S(1)}) custom-call(s32[4,16]{1,0:T(4,128)S(1)} %get-tuple-element.36.owners, bf16[256,2048]{1,0:T(8,128)(2,1)} %get-tuple-element.37.q_in, bf16[256,2048]{1,0:T(8,128)(2,1)} %get-tuple-element.38.k_in, ...), custom_call_target="tpu_custom_call" | custom-call | tf_op jit(solution)/shard_map/cond/branch_0_fun/slots4/pallas_call | solution.py:333
  80.9 1.0 %copy.30 = bf16[256,2048]{1,0:T(8,128)(2,1)} copy(bf16[256,2048]{1,0:T(8,128)(2,1)S(1)} %get-tuple-element.83) | data formatting | bytes 2097152
  81.8 1.0 %copy.31 = bf16[256,2048]{1,0:T(8,128)(2,1)} copy(bf16[256,2048]{1,0:T(8,128)(2,1)S(1)} %get-tuple-element.84) | data formatting | bytes 2097152
  82.8 1.0 %copy.32 = bf16[256,2048]{1,0:T(8,128)(2,1)} copy(bf16[256,2048]{1,0:T(8,128)(2,1)S(1)} %get-tuple-element.85) | data formatting | bytes 2097152
  (2 shorter events, 0.0 us)
Async XLA Ops:
  0.7 0.7 copy-start

commit v2 on v1

v2 whole, which is shorter than its diff:
```python
import functools
import math

import jax
import jax.numpy as jnp
from jax import lax
from jax.experimental import pallas as pl
from jax.experimental.pallas import tpu as pltpu
from jax.sharding import PartitionSpec as P

HD = 128
BLK = 128
SL = 256
MESH = pl.DeviceIdType.MESH
F32 = jnp.float32
BF16 = jnp.bfloat16
NEG = -1e30
LEAD, QUERY_LAG, KEY_LAG = 2, 1, 2
KEY, VAL, QRY, GRD, OUT = range(5)


def dot(a, b, dims):
    return lax.dot_general(a, b, (dims, ((), ())), preferred_element_type=F32)


def kernel(w, nh, owners, q_in, k_in, v_in, o_in, g_in, dq_out, dk_out, dv_out,
           own, kv_out, kv_in, qg_out, qg_in, stat_out, stat_near, stat_far, part_own, stage,
           s_buf, dp_buf, p_buf, ds_buf, sk_buf, dpk_buf, pk_buf, dsk_buf,
           loc_sem, xs_sem, xr_sem, kas_sem, kar_sem, kbs_sem, kbr_sem, qas_sem, qar_sem, qbs_sem, qbr_sem,
           sns_sem, snr_sem, sfs_sem, sfr_sem, ol_sem, os_sem, or_sem):
    n_seq = lax.axis_size("seq")
    n_all = lax.axis_size("grp") * n_seq
    me = lax.axis_index("grp") * n_seq + lax.axis_index("seq")
    core = lax.rem(me, 2)
    even = me - core
    na = w - 2

    def dev(d):
        d = lax.rem(d + n_all, n_all)
        return (d // n_seq, lax.rem(d, n_seq))

    def only(cond):
        return lambda act: pl.when(cond)(act)

    mate = dev(even + 1 - core)
    ahead, ahead_two, behind, behind_two = [dev(me + i) for i in (2, 4, -2, -4)]
    has_ahead, has_ahead_two = me < n_all - 2, me < n_all - 4
    has_behind, has_behind_two = me >= 2, me >= 4
    when_ahead, when_ahead_two = only(has_ahead), only(has_ahead_two)
    when_behind, when_behind_two = only(has_behind), only(has_behind_two)

    barrier = pltpu.get_barrier_semaphore()
    pl.semaphore_signal(barrier, inc=1, device_id=mate, device_id_type=MESH)
    met = jnp.int32(1)
    for there, other in ((has_ahead, ahead), (has_behind, behind), (has_ahead_two, ahead_two), (has_behind_two, behind_two)):
        @pl.when(there)
        def _():
            pl.semaphore_signal(barrier, inc=1, device_id=other, device_id_type=MESH)

        met += there.astype(jnp.int32)

    inputs = (k_in, v_in, q_in, g_in, o_in)
    outputs = (dq_out, dk_out, dv_out)

    def cols(which_core, h):
        return pl.ds(pl.multiple_of((which_core * nh + h) * HD, HD), HD)

    mine = pl.ds(pl.multiple_of(core * SL, SL), SL)
    mates = pl.ds(pl.multiple_of((1 - core) * SL, SL), SL)

    def local_in(h, a):
        return pltpu.make_async_copy(inputs[a].at[:, cols(core, h)], own.at[h, a, mine], loc_sem.at[h, a])

    def mate_in(h, a):
        return pltpu.make_async_remote_copy(
            src_ref=inputs[a].at[:, cols(1 - core, h)], dst_ref=own.at[h, a, mine],
            send_sem=xs_sem.at[h, a], recv_sem=xr_sem.at[h, a], device_id=mate, device_id_type=MESH)

    def mate_in_arrival(h, a):
        return pltpu.make_async_remote_copy(
            src_ref=own.at[h, a, mates], dst_ref=own.at[h, a, mates],
            send_sem=xs_sem.at[h, a], recv_sem=xr_sem.at[h, a], device_id=mate, device_id_type=MESH)

    def hop(src, dst, h, lo, size, ss, rs, to):
        return pltpu.make_async_remote_copy(
            src_ref=src.at[h, pl.ds(lo, size)], dst_ref=dst.at[h, pl.ds(lo, size)],
            send_sem=ss.at[h], recv_sem=rs.at[h], device_id=to, device_id_type=MESH)

    def keys_a(h):
        return hop(kv_out, kv_in, h, 0, na, kas_sem, kar_sem, ahead)

    def keys_b(h):
        return hop(kv_out, kv_in, h, na, 2, kbs_sem, kbr_sem, ahead)

    def rows_a(h):
        return hop(qg_out, qg_in, h, 0, na, qas_sem, qar_sem, behind)

    def rows_b(h):
        return hop(qg_out, qg_in, h, na, 2, qbs_sem, qbr_sem, behind)

    def stats_near(h):
        return hop(stat_out, stat_near, h, 0, 16, sns_sem, snr_sem, behind)

    def stats_far(h):
        return hop(stat_out, stat_far, h, 0, 16, sfs_sem, sfr_sem, behind_two)

    def local_res(h, a):
        return pltpu.make_async_copy(stage.at[h, a, mine], outputs[a].at[:, cols(core, h)], ol_sem.at[h, a])

    def mate_res(h, a):
        return pltpu.make_async_remote_copy(
            src_ref=stage.at[h, a, mates], dst_ref=outputs[a].at[:, cols(core, h)],
            send_sem=os_sem.at[h, a], recv_sem=or_sem.at[h, a], device_id=mate, device_id_type=MESH)

    def mate_res_arrival(h, a):
        return pltpu.make_async_remote_copy(
            src_ref=stage.at[h, a, mates], dst_ref=outputs[a].at[:, cols(1 - core, h)],
            send_sem=os_sem.at[h, a], recv_sem=or_sem.at[h, a], device_id=mate, device_id_type=MESH)

    def live_count(shard):
        s = jnp.clip(shard, 0, n_all - 1)
        total = jnp.int32(0)
        for b in range(owners.shape[1]):
            total += (owners[s // n_seq, b] == lax.rem(s, n_seq)).astype(jnp.int32)
        return jnp.where(jnp.logical_and(shard >= 0, shard < n_all), total, 0)

    c_m3, c_m2, c_m1, c_e, c_o, c_p2, c_p3, c_p4 = [live_count(even + i) for i in range(-3, 5)]
    own_live = (c_e >= 1, c_e >= 2, c_o >= 1, c_o >= 2)

    def arrivals(passed_count, own_count):
        passed, there = [], []
        for t in range(w):
            by_pass = jnp.bool_(False)
            if t == w - 1:
                by_pass = passed_count >= 1
            elif t == w - 2:
                by_pass = passed_count >= 2
            passed.append(by_pass)
            there.append(jnp.logical_and(jnp.logical_not(by_pass), own_count > t))
        return passed, there

    key_passed, key_own = arrivals(c_m3, c_m1 + c_m2)
    row_passed, row_own = arrivals(c_p4, c_p2 + c_p3)

    def fetch(h, a_list):
        for a in a_list:
            local_in(h, a).start()
            mate_in(h, a).start()

    def fetched(h, a_list):
        for a in a_list:
            local_in(h, a).wait()
            mate_in_arrival(h, a).wait_recv()

    def numbered(t, first_count, first, then):
        if t == 0:
            return jnp.where(first_count >= 1, first(0), then(0))
        if t == 1:
            return jnp.where(first_count >= 2, first(1), jnp.where(first_count >= 1, then(0), then(1)))
        if t == 2:
            return jnp.where(first_count >= 2, then(0), then(1))
        return then(1)

    def own_pick(h, x, t):
        def from_even(i):
            return own[h, x, i * BLK:(i + 1) * BLK, :]

        def from_odd(i):
            return own[h, x, (2 + i) * BLK:(3 + i) * BLK, :]

        if x in (KEY, VAL):
            return numbered(t, c_o, from_odd, from_even)
        return numbered(t, c_e, from_even, from_odd)

    def make_a(h, pair, out):
        for t in range(na):
            for i, x in enumerate(pair):
                out[h, t, i] = own_pick(h, x, t)

    def make_b(h, pair, arrived, out, passed_count):
        for i, x in enumerate(pair):
            first, second = arrived[h, 0, i], arrived[h, 1, i]
            if w - 2 < 4:
                second = jnp.where(passed_count >= 2, second, own_pick(h, x, w - 2))
            if w - 1 < 4:
                first = jnp.where(passed_count >= 1, first, own_pick(h, x, w - 1))
            out[h, w - 2, i] = second
            out[h, w - 1, i] = first

    inv_root = HD ** (-0.5)
    exp_scale = inv_root * math.log2(math.e)
    row_id = lax.broadcasted_iota(jnp.int32, (BLK, SL), 0)
    col_id = lax.broadcasted_iota(jnp.int32, (BLK, SL), 1)
    first_half = lax.broadcasted_iota(jnp.int32, (1, SL), 1) < BLK
    nat, both_last = ((1,), (0,)), ((1,), (1,))

    def block(b):
        return slice(b * BLK, (b + 1) * BLK)

    def query_side(h):
        keys, vals = own[h, KEY], own[h, VAL]
        far_keys = kv_in[h, :, 0].reshape(w * BLK, HD)
        far_vals = kv_in[h, :, 1].reshape(w * BLK, HD)
        prod = own[h, GRD].astype(F32) * own[h, OUT].astype(F32)
        delta_all = jnp.sum(prod.T, axis=0, keepdims=True)
        for a in range(2):
            nk = SL * (a + 1)
            rows = slice(a * SL, (a + 1) * SL)
            query, grad = own[h, QRY, rows], own[h, GRD, rows]
            delta = delta_all[:, rows]
            s_buf[0:nk] = dot(keys[:nk], query, both_last)
            s_buf[2 * SL:] = dot(far_keys, query, both_last)
            dp_buf[0:nk] = dot(vals[:nk], grad, both_last)
            dp_buf[2 * SL:] = dot(far_vals, grad, both_last)
            blocks = list(range(nk // BLK)) + [4 + t for t in range(w)]
            top = None
            for b in blocks:
                if b >= 4:
                    ok = key_own[b - 4]
                    if a == 0:
                        ok = jnp.logical_or(ok, key_passed[b - 4])
                else:
                    ok = own_live[b]
                x = s_buf[block(b)] + jnp.where(ok, 0.0, NEG).astype(F32)
                if b < 4 and b >= 2 * a:
                    x = jnp.where(row_id + (b - 2 * a) * BLK <= col_id, x, NEG)
                s_buf[block(b)] = x
                high = jnp.max(x, axis=0, keepdims=True)
                top = high if top is None else jnp.maximum(top, high)
            total = None
            for b in blocks:
                e = jnp.exp2((s_buf[block(b)] - top) * exp_scale)
                s_buf[block(b)] = e
                part = jnp.sum(e, axis=0, keepdims=True)
                total = part if total is None else total + part
            live = jnp.where(first_half, jnp.where(own_live[2 * a], 1.0, 0.0).astype(F32),
                             jnp.where(own_live[2 * a + 1], 1.0, 0.0).astype(F32))
            scale = live / total
            for i in range(2):
                for r, stat in enumerate((top, scale, delta)):
                    stat_out[h, 4 * r + 2 * a + i:4 * r + 2 * a + i + 1, :] = stat[:, block(i)]
            for b in blocks:
                prob = s_buf[block(b)] * scale
                if b < 4:
                    p_buf[block(b), rows] = prob.astype(BF16)
                ds_buf[block(b), rows] = (prob * (dp_buf[block(b)] - delta)).astype(BF16)
            dq = dot(ds_buf[0:nk, rows], keys[:nk], ((0,), (0,)))
            dq += dot(ds_buf[2 * SL:, rows], far_keys, ((0,), (0,)))
            stage[h, 0, rows] = (dq * inv_root).astype(BF16)

    def own_keys(h):
        second = slice(SL, 2 * SL)
        query, grad = own[h, QRY], own[h, GRD]
        part_own[h, 0, 0:SL] = dot(ds_buf[0:SL], query, nat)
        part_own[h, 0, second] = dot(ds_buf[second, second], query[second], nat)
        part_own[h, 1, 0:SL] = dot(p_buf[0:SL], grad, nat)
        part_own[h, 1, second] = dot(p_buf[second, second], grad[second], nat)

    def key_side(h):
        queries = qg_in[h, :, 0].reshape(w * BLK, HD)
        grads = qg_in[h, :, 1].reshape(w * BLK, HD)
        sk_buf[...] = dot(own[h, KEY], queries, both_last)
        dpk_buf[...] = dot(own[h, VAL], grads, both_last)
        for t in range(w):
            def stat(r):
                def near(i):
                    return stat_near[h, 4 * r + i:4 * r + i + 1, :]

                row = numbered(t, c_p2, near, lambda i: near(2 + i))
                if t == w - 1:
                    row = jnp.where(row_passed[t], stat_far[h, 4 * r:4 * r + 1, :], row)
                if t == w - 2:
                    row = jnp.where(row_passed[t], stat_far[h, 4 * r + 1:4 * r + 2, :], row)
                return row

            top, scale, delta = stat(0), stat(1), stat(2)
            for b in range(4):
                ok = row_own[t]
                if b >= 2:
                    ok = jnp.logical_or(ok, row_passed[t])
                level = jnp.where(jnp.logical_and(ok, own_live[b]), top, -NEG)
                prob = jnp.exp2((sk_buf[block(b), block(t)] - level) * exp_scale) * scale
                pk_buf[block(b), block(t)] = prob.astype(BF16)
                dsk_buf[block(b), block(t)] = (prob * (dpk_buf[block(b), block(t)] - delta)).astype(BF16)
        dk = part_own[h, 0] + dot(dsk_buf[...], queries, nat)
        stage[h, 1] = (dk * inv_root).astype(BF16)
        stage[h, 2] = (part_own[h, 1] + dot(pk_buf[...], grads, nat)).astype(BF16)

    early = min(LEAD, nh)
    for h in range(early):
        for a in (KEY, VAL, QRY, GRD):
            local_in(h, a).start()

    @pl.when(jnp.logical_not(has_behind))
    def _():
        kv_in[...] = jnp.zeros_like(kv_in)

    @pl.when(jnp.logical_not(has_ahead))
    def _():
        qg_in[...] = jnp.zeros_like(qg_in)
        stat_near[...] = jnp.zeros_like(stat_near)

    @pl.when(jnp.logical_not(has_ahead_two))
    def _():
        stat_far[...] = jnp.zeros_like(stat_far)

    pl.semaphore_wait(barrier, met)
    for h in range(early):
        for a in (KEY, VAL, QRY, GRD):
            mate_in(h, a).start()

    def start_a(h):
        fetched(h, (KEY, VAL))

        @when_ahead
        def _():
            make_a(h, (KEY, VAL), kv_out)
            keys_a(h).start()

        fetched(h, (QRY, GRD))

        @when_behind
        def _():
            make_a(h, (QRY, GRD), qg_out)
            rows_a(h).start()

    for h in range(early):
        start_a(h)

    for h in range(early):
        fetch(h, (OUT,))

    @pl.loop(early, nh)
    def _(h):
        fetch(h, (KEY, VAL, QRY, GRD, OUT))

    @pl.loop(0, nh + KEY_LAG)
    def _(step):
        @pl.when(step < nh)
        def _():
            h = step

            @when_behind
            def _():
                keys_a(h).wait_recv()

            @when_ahead
            def _():
                make_b(h, (KEY, VAL), kv_in, kv_out, c_m1)
                keys_b(h).start()
                rows_a(h).wait_recv()

            @when_behind
            def _():
                make_b(h, (QRY, GRD), qg_in, qg_out, c_p2)
                rows_b(h).start()

        @pl.when(step + early < nh)
        def _():
            start_a(step + early)

        @pl.when(jnp.logical_and(step >= QUERY_LAG, step < nh + QUERY_LAG))
        def _():
            h = step - QUERY_LAG
            fetched(h, (OUT,))

            @when_behind
            def _():
                keys_b(h).wait_recv()

            query_side(h)

            @when_behind
            def _():
                stats_near(h).start()

            @when_behind_two
            def _():
                stats_far(h).start()

            local_res(h, 0).start()
            mate_res(h, 0).start()
            own_keys(h)

        @pl.when(step >= KEY_LAG)
        def _():
            h = step - KEY_LAG

            @when_ahead
            def _():
                rows_b(h).wait_recv()
                stats_near(h).wait_recv()

            @when_ahead_two
            def _():
                stats_far(h).wait_recv()

            key_side(h)
            for a in (1, 2):
                local_res(h, a).start()
                mate_res(h, a).start()

    @pl.loop(0, nh)
    def _(h):
        for a in range(5):
            mate_in(h, a).wait_send()

        @when_ahead
        def _():
            keys_a(h).wait_send()
            keys_b(h).wait_send()

        @when_behind
        def _():
            rows_a(h).wait_send()
            rows_b(h).wait_send()
            stats_near(h).wait_send()

        @when_behind_two
        def _():
            stats_far(h).wait_send()

        for a in range(3):
            local_res(h, a).wait()
            mate_res(h, a).wait_send()
            mate_res_arrival(h, a).wait_recv()


def fused(w, owners, queries, key_states, value_states, attn_out, out_grad):
    width = queries.shape[1]
    nh = width // (2 * HD)
    anywhere = pl.BlockSpec(memory_space=pl.ANY)
    dma = pltpu.SemaphoreType.DMA
    slots = pltpu.VMEM((nh, w, 2, BLK, HD), BF16)
    stats = pltpu.VMEM((nh, 16, HD), F32)
    return pl.pallas_call(
        functools.partial(kernel, w, nh),
        out_shape=[jax.ShapeDtypeStruct(queries.shape, BF16)] * 3,
        in_specs=[pl.BlockSpec(memory_space=pltpu.SMEM)] + [anywhere] * 5,
        out_specs=[anywhere] * 3,
        scratch_shapes=[
            pltpu.VMEM((nh, 5, 2 * SL, HD), BF16),
            slots, slots, slots, slots,
            stats, stats, stats,
            pltpu.VMEM((nh, 2, 2 * SL, HD), F32),
            pltpu.VMEM((nh, 3, 2 * SL, HD), BF16),
            pltpu.VMEM(((4 + w) * BLK, SL), F32),
            pltpu.VMEM(((4 + w) * BLK, SL), F32),
            pltpu.VMEM((2 * SL, 2 * SL), BF16),
            pltpu.VMEM(((4 + w) * BLK, 2 * SL), BF16),
            pltpu.VMEM((2 * SL, w * BLK), F32),
            pltpu.VMEM((2 * SL, w * BLK), F32),
            pltpu.VMEM((2 * SL, w * BLK), BF16),
            pltpu.VMEM((2 * SL, w * BLK), BF16),
            dma((nh, 5)), dma((nh, 5)), dma((nh, 5)),
        ] + [dma((nh,))] * 12 + [dma((nh, 3))] * 3,
        compiler_params=pltpu.CompilerParams(
            collective_id=w - 4, has_side_effects=True, vmem_limit_bytes=56 * 2**20),
        name="slots%d" % w,
    )(owners, queries, key_states, value_states, attn_out, out_grad)


def per_device(queries, key_states, value_states, attn_out, out_grad, owner_ids):
    n_grp, n_seq = lax.axis_size("grp"), lax.axis_size("seq")
    shard = (owner_ids + n_seq * jnp.arange(n_grp, dtype=jnp.int32)[:, None]).reshape(-1)
    last = shard + 2 - jnp.logical_or(shard == 0, shard == n_grp * n_seq - 3).astype(jnp.int32)
    five = (shard[4:] <= last[:-4]).astype(jnp.int32)
    six = (jnp.pad(shard[5:], (0, 1), constant_values=n_grp * n_seq + 2) <= last[:-4]).astype(jnp.int32)
    return lax.switch(
        jnp.max(five + six),
        [functools.partial(fused, w) for w in (4, 5, 6)],
        owner_ids, queries, key_states, value_states, attn_out, out_grad)


def solution(mesh):
    rows = P(("grp", "seq"), None)
    return jax.shard_map(
        per_device,
        mesh=mesh,
        in_specs=(rows,) * 5 + (P(),),
        out_specs=(rows,) * 3,
        check_vma=False,
    )
```

time: 84 us -> 101 us (1.20)
  the two profiles are of different devices: /device:TPU:1 before, /device:TPU:7 now
where the time goes in v2:
time: 101 us; the launch traced here: 100 us
  Pallas kernels  94.3 us (93%)
  local copies, waits for them, and re-layouts  3.74 us (4%)
  between operations  1.31 us (1%)
    pallas_call x1, Pallas kernels, fused(): pl.pallas_call(functools.partial(kernel, w, nh), out_shape=[jax.ShapeDtyp...  94.3 us
    unnamed x5, local copies, waits for them, and re-layouts  3.58 us

profile of v2, /device:TPU:7, one launch (start us, length us, event | category | flops | bytes accessed | tf_op | source)
XLA Modules:
  0.0 100.4 jit_solution(5434349093834651570)
XLA Ops:
  0.6 0.0 copy-start
  0.7 0.7 copy-done
  1.3 0.1 broadcast_add_fusion
  1.4 0.1 reshape.14
  1.5 0.1 slice.12
  1.5 0.7 fusion.2
  2.9 94.6 %conditional.1 = ((bf16[256,2048]{1,0:T(8,128)(2,1)S(1)}, bf16[256,2048]{1,0:T(8,128)(2,1)S(1)}, bf16[256,2048]{1,0:T(8,128)(2,1)S(1)})) conditional(s32[]{:T(128)} %clamp.3, (s32[4,16]{1,0:T(4,128)S(1)}, bf16[256,2048]{1,0:T(8,128)(2,1)}, bf16[256,2048]{1,0:T(8,128)(2,1)}, bf16[256,2048]{1,0:T(8,128)(2,1)}, ...), branch_computations={%region_1.2_spmd, %region_2.3_spmd, %region_3.4_spmd} | conditional | bytes 8 | solution.py:469
  2.9 94.3 %slots6.1 = (bf16[256,2048]{1,0:T(8,128)(2,1)S(1)}, bf16[256,2048]{1,0:T(8,128)(2,1)S(1)}, bf16[256,2048]{1,0:T(8,128)(2,1)S(1)}) custom-call(s32[4,16]{1,0:T(4,128)S(1)} %get-tuple-element.48.owners, bf16[256,2048]{1,0:T(8,128)(2,1)} %get-tuple-element.49.q_in, bf16[256,2048]{1,0:T(8,128)(2,1)} %get-tuple-element.50.k_in, ...), custom_call_target="tpu_custom_call" | custom-call | tf_op jit(solution)/shard_map/cond/branch_2_fun/slots6/pallas_call | solution.py:436
  97.5 1.0 copy.30
  98.5 1.0 copy.31
  99.4 1.0 copy.32
  (2 shorter events, 0.0 us)
Async XLA Ops:
  0.6 0.7 copy-start

commit v3 on v2

--- a/solution.py
+++ b/solution.py
@@ -15,7 +15,7 @@
 F32 = jnp.float32
 BF16 = jnp.bfloat16
 NEG = -1e30
-LEAD, QUERY_LAG, KEY_LAG = 2, 1, 2
+LEAD, QUERY_LAG, KEY_LAG = 2, 1, 3
 KEY, VAL, QRY, GRD, OUT = range(5)
 
 
@@ -359,29 +359,6 @@
         def _():
             start_a(step + early)
 
-        @pl.when(jnp.logical_and(step >= QUERY_LAG, step < nh + QUERY_LAG))
-        def _():
-            h = step - QUERY_LAG
-            fetched(h, (OUT,))
-
-            @when_behind
-            def _():
-                keys_b(h).wait_recv()
-
-            query_side(h)
-
-            @when_behind
-            def _():
-                stats_near(h).start()
-
-            @when_behind_two
-            def _():
-                stats_far(h).start()
-
-            local_res(h, 0).start()
-            mate_res(h, 0).start()
-            own_keys(h)
-
         @pl.when(step >= KEY_LAG)
         def _():
             h = step - KEY_LAG
@@ -399,6 +376,29 @@
             for a in (1, 2):
                 local_res(h, a).start()
                 mate_res(h, a).start()
+
+        @pl.when(jnp.logical_and(step >= QUERY_LAG, step < nh + QUERY_LAG))
+        def _():
+            h = step - QUERY_LAG
+            fetched(h, (OUT,))
+
+            @when_behind
+            def _():
+                keys_b(h).wait_recv()
+
+            query_side(h)
+
+            @when_behind
+            def _():
+                stats_near(h).start()
+
+            @when_behind_two
+            def _():
+                stats_far(h).start()
+
+            local_res(h, 0).start()
+            mate_res(h, 0).start()
+            own_keys(h)
 
     @pl.loop(0, nh)
     def _(h):
@@ -460,16 +460,32 @@
     )(owners, queries, key_states, value_states, attn_out, out_grad)
 
 
+def place(a, b, c, x, y, z, sems):
+    copies = [pltpu.make_async_copy(s, d, sems.at[i]) for i, (s, d) in enumerate(((a, x), (b, y), (c, z)))]
+    for copy in copies:
+        copy.start()
+    for copy in copies:
+        copy.wait()
+
+
+def placed(arrays):
+    anywhere = pl.BlockSpec(memory_space=pl.ANY)
+    return pl.pallas_call(
+        place, out_shape=[jax.ShapeDtypeStruct(a.shape, a.dtype) for a in arrays],
+        in_specs=[anywhere] * 3, out_specs=[anywhere] * 3,
+        scratch_shapes=[pltpu.SemaphoreType.DMA((3,))], name="place")(*arrays)
+
+
 def per_device(queries, key_states, value_states, attn_out, out_grad, owner_ids):
     n_grp, n_seq = lax.axis_size("grp"), lax.axis_size("seq")
     shard = (owner_ids + n_seq * jnp.arange(n_grp, dtype=jnp.int32)[:, None]).reshape(-1)
     last = shard + 2 - jnp.logical_or(shard == 0, shard == n_grp * n_seq - 3).astype(jnp.int32)
     five = (shard[4:] <= last[:-4]).astype(jnp.int32)
     six = (jnp.pad(shard[5:], (0, 1), constant_values=n_grp * n_seq + 2) <= last[:-4]).astype(jnp.int32)
-    return lax.switch(
+    return placed(lax.switch(
         jnp.max(five + six),
         [functools.partial(fused, w) for w in (4, 5, 6)],
-        owner_ids, queries, key_states, value_states, attn_out, out_grad)
+        owner_ids, queries, key_states, value_states, attn_out, out_grad))
 
 
 def solution(mesh):

time: 101 us -> 71.7 us (0.71)
  Pallas kernels: 94.3 us -> 68.1 us
  local copies, waits for them, and re-layouts: 3.74 us -> 0.82 us
    pallas_call x1, Pallas kernels: 94.3 us -> 66.4 us  [fused(): pl.pallas_call(functools.partial(kernel, w, nh), out_shape=[jax.ShapeDtyp...]
    unnamed x5 -> x2, local copies, waits for them, and re-layouts: 3.58 us -> 0.66 us
    pallas_call x0 -> x1, Pallas kernels: none -> 1.69 us  [placed(): pl.pallas_call(place, out_shape=[jax.ShapeDtypeStruct(a.shape, a.dtype) f...]
where the time goes in v3:
time: 71.7 us; the launch traced here: 71.4 us
  Pallas kernels  68.1 us (95%)
  between operations  1.49 us (2%)
  local copies, waits for them, and re-layouts  0.82 us (1%)
  other arithmetic  0.78 us (1%)
    pallas_call x1, Pallas kernels, fused(): pl.pallas_call(functools.partial(kernel, w, nh), out_shape=[jax.ShapeDtyp...  66.4 us
    pallas_call x1, Pallas kernels, placed(): pl.pallas_call(place, out_shape=[jax.ShapeDtypeStruct(a.shape, a.dtype) f...  1.69 us

profile of v3, /device:TPU:7, one launch (start us, length us, event | category | flops | bytes accessed | tf_op | source)
XLA Modules:
  0.0 71.4 jit_solution(3829789949855389307)
XLA Ops:
  0.6 0.0 copy-start
  0.7 0.7 copy-done
  1.3 0.1 broadcast_add_fusion
  1.4 0.1 reshape.14
  1.5 0.1 slice.12
  1.5 0.7 fusion.2
  2.9 66.6 %conditional.1 = ((bf16[256,2048]{1,0:T(8,128)(2,1)S(1)}, bf16[256,2048]{1,0:T(8,128)(2,1)S(1)}, bf16[256,2048]{1,0:T(8,128)(2,1)S(1)})) conditional(s32[]{:T(128)} %clamp.3, (s32[4,16]{1,0:T(4,128)S(1)}, bf16[256,2048]{1,0:T(8,128)(2,1)}, bf16[256,2048]{1,0:T(8,128)(2,1)}, bf16[256,2048]{1,0:T(8,128)(2,1)}, ...), branch_computations={%region_1.2_spmd, %region_2.3_spmd, %region_3.4_spmd} | conditional | bytes 8 | solution.py:485
  2.9 66.4 %slots4.1 = (bf16[256,2048]{1,0:T(8,128)(2,1)S(1)}, bf16[256,2048]{1,0:T(8,128)(2,1)S(1)}, bf16[256,2048]{1,0:T(8,128)(2,1)S(1)}) custom-call(s32[4,16]{1,0:T(4,128)S(1)} %get-tuple-element.36.owners, bf16[256,2048]{1,0:T(8,128)(2,1)} %get-tuple-element.37.q_in, bf16[256,2048]{1,0:T(8,128)(2,1)} %get-tuple-element.38.k_in, ...), custom_call_target="tpu_custom_call" | custom-call | tf_op jit(solution)/shard_map/cond/branch_0_fun/slots4/pallas_call | solution.py:436
  69.5 1.7 %place.1 = (bf16[256,2048]{1,0:T(8,128)(2,1)}, bf16[256,2048]{1,0:T(8,128)(2,1)}, bf16[256,2048]{1,0:T(8,128)(2,1)}) custom-call(bf16[256,2048]{1,0:T(8,128)(2,1)S(1)} %get-tuple-element.60.a, bf16[256,2048]{1,0:T(8,128)(2,1)S(1)} %get-tuple-element.61.b, bf16[256,2048]{1,0:T(8,128)(2,1)S(1)} %get-tuple-element.62.c), custom_call_target="tpu_custom_call" | custom-call | tf_op jit(solution)/shard_map/place/pallas_call | solution.py:473
  (2 shorter events, 0.0 us)
Async XLA Ops:
  0.6 0.7 copy-start

commit v4 on v3

--- a/solution.py
+++ b/solution.py
@@ -15,7 +15,7 @@
 F32 = jnp.float32
 BF16 = jnp.bfloat16
 NEG = -1e30
-LEAD, QUERY_LAG, KEY_LAG = 2, 1, 3
+LEAD, QUERY_LAG, KEY_LAG, DRAIN_LAG = 2, 1, 3, 5
 KEY, VAL, QRY, GRD, OUT = range(5)
 
 
@@ -23,10 +23,16 @@
     return lax.dot_general(a, b, (dims, ((), ())), preferred_element_type=F32)
 
 
-def kernel(w, nh, owners, q_in, k_in, v_in, o_in, g_in, dq_out, dk_out, dv_out,
+def needs(far, first, second, next_one, next_two, next_three):
+    near_two = next_one + next_two
+    return (jnp.where(next_one > 0, far, 0), jnp.where(near_two > 0, first, 0),
+            jnp.where(near_two + next_three > 0, second, 0))
+
+
+def kernel(w, nh, owners_in, q_in, k_in, v_in, o_in, g_in, dq_out, dk_out, dv_out,
            own, kv_out, kv_in, qg_out, qg_in, stat_out, stat_near, stat_far, part_own, stage,
            s_buf, dp_buf, p_buf, ds_buf, sk_buf, dpk_buf, pk_buf, dsk_buf,
-           loc_sem, xs_sem, xr_sem, kas_sem, kar_sem, kbs_sem, kbr_sem, qas_sem, qar_sem, qbs_sem, qbr_sem,
+           owners, owners_sem, loc_sem, xs_sem, xr_sem, kas_sem, kar_sem, kbs_sem, kbr_sem, qas_sem, qar_sem, qbs_sem, qbr_sem,
            sns_sem, snr_sem, sfs_sem, sfr_sem, ol_sem, os_sem, or_sem):
     n_seq = lax.axis_size("seq")
     n_all = lax.axis_size("grp") * n_seq
@@ -59,6 +65,9 @@
 
         met += there.astype(jnp.int32)
 
+    owners_copy = pltpu.make_async_copy(owners_in, owners, owners_sem)
+    owners_copy.start()
+
     inputs = (k_in, v_in, q_in, g_in, o_in)
     outputs = (dq_out, dk_out, dv_out)
 
@@ -89,8 +98,10 @@
     def keys_a(h):
         return hop(kv_out, kv_in, h, 0, na, kas_sem, kar_sem, ahead)
 
-    def keys_b(h):
-        return hop(kv_out, kv_in, h, na, 2, kbs_sem, kbr_sem, ahead)
+    def keys_b(h, i):
+        return pltpu.make_async_remote_copy(
+            src_ref=kv_out.at[h, pl.ds(na, 2), i], dst_ref=kv_in.at[h, pl.ds(na, 2), i],
+            send_sem=kbs_sem.at[h, i], recv_sem=kbr_sem.at[h, i], device_id=ahead, device_id_type=MESH)
 
     def rows_a(h):
         return hop(qg_out, qg_in, h, 0, na, qas_sem, qar_sem, behind)
@@ -116,6 +127,10 @@
         return pltpu.make_async_remote_copy(
             src_ref=stage.at[h, a, mates], dst_ref=outputs[a].at[:, cols(1 - core, h)],
             send_sem=os_sem.at[h, a], recv_sem=or_sem.at[h, a], device_id=mate, device_id_type=MESH)
+
+    def give(h, a):
+        local_res(h, a).start()
+        mate_res(h, a).start()
 
     def live_count(shard):
         s = jnp.clip(shard, 0, n_all - 1)
@@ -124,8 +139,19 @@
             total += (owners[s // n_seq, b] == lax.rem(s, n_seq)).astype(jnp.int32)
         return jnp.where(jnp.logical_and(shard >= 0, shard < n_all), total, 0)
 
-    c_m3, c_m2, c_m1, c_e, c_o, c_p2, c_p3, c_p4 = [live_count(even + i) for i in range(-3, 5)]
-    own_live = (c_e >= 1, c_e >= 2, c_o >= 1, c_o >= 2)
+    early = min(LEAD, nh)
+    for h in range(early):
+        for a in (KEY, VAL, QRY, GRD):
+            local_in(h, a).start()
+
+    owners_copy.wait()
+    m3, m2, m1, e0, o0, p2, p3, p4 = [live_count(even + i) for i in range(-3, 5)]
+    own_live = (e0 >= 1, e0 >= 2, o0 >= 1, o0 >= 2)
+
+    key_from_far, key_from_even, key_from_odd = needs(m3, m2, m1, e0, o0, p2)
+    key_pass, key_even, key_odd = needs(m1, e0, o0, p2, p3, p4)
+    row_from_far, row_from_odd, row_from_even = needs(p4, p3, p2, o0, e0, m1)
+    row_pass, row_odd, row_even = needs(p2, o0, e0, m1, m2, m3)
 
     def arrivals(passed_count, own_count):
         passed, there = [], []
@@ -139,8 +165,8 @@
             there.append(jnp.logical_and(jnp.logical_not(by_pass), own_count > t))
         return passed, there
 
-    key_passed, key_own = arrivals(c_m3, c_m1 + c_m2)
-    row_passed, row_own = arrivals(c_p4, c_p2 + c_p3)
+    key_passed, key_own = arrivals(key_from_far, key_from_even + key_from_odd)
+    row_passed, row_own = arrivals(row_from_far, row_from_even + row_from_odd)
 
     def fetch(h, a_list):
         for a in a_list:
@@ -169,8 +195,8 @@
             return own[h, x, (2 + i) * BLK:(3 + i) * BLK, :]
 
         if x in (KEY, VAL):
-            return numbered(t, c_o, from_odd, from_even)
-        return numbered(t, c_e, from_even, from_odd)
+            return numbered(t, key_odd, from_odd, from_even)
+        return numbered(t, row_even, from_even, from_odd)
 
     def make_a(h, pair, out):
         for t in range(na):
@@ -197,22 +223,22 @@
     def block(b):
         return slice(b * BLK, (b + 1) * BLK)
 
-    def query_side(h):
-        keys, vals = own[h, KEY], own[h, VAL]
+    def half(a):
+        return 2 * (a + 1), slice(a * SL, (a + 1) * SL)
+
+    def soft_part(h):
+        keys = own[h, KEY]
         far_keys = kv_in[h, :, 0].reshape(w * BLK, HD)
-        far_vals = kv_in[h, :, 1].reshape(w * BLK, HD)
         prod = own[h, GRD].astype(F32) * own[h, OUT].astype(F32)
         delta_all = jnp.sum(prod.T, axis=0, keepdims=True)
         for a in range(2):
-            nk = SL * (a + 1)
-            rows = slice(a * SL, (a + 1) * SL)
-            query, grad = own[h, QRY, rows], own[h, GRD, rows]
-            delta = delta_all[:, rows]
-            s_buf[0:nk] = dot(keys[:nk], query, both_last)
-            s_buf[2 * SL:] = dot(far_keys, query, both_last)
-            dp_buf[0:nk] = dot(vals[:nk], grad, both_last)
-            dp_buf[2 * SL:] = dot(far_vals, grad, both_last)
-            blocks = list(range(nk // BLK)) + [4 + t for t in range(w)]
+            near, rows = half(a)
+            query = own[h, QRY, rows]
+            s_buf[0:near * BLK, rows] = dot(keys[:near * BLK], query, both_last)
+            s_buf[4 * BLK:, rows] = dot(far_keys, query, both_last)
+        for a in range(2):
+            near, rows = half(a)
+            blocks = list(range(near)) + [4 + t for t in range(w)]
             top = None
             for b in blocks:
                 if b >= 4:
@@ -221,31 +247,44 @@
                         ok = jnp.logical_or(ok, key_passed[b - 4])
                 else:
                     ok = own_live[b]
-                x = s_buf[block(b)] + jnp.where(ok, 0.0, NEG).astype(F32)
+                x = s_buf[block(b), rows] + jnp.where(ok, 0.0, NEG).astype(F32)
                 if b < 4 and b >= 2 * a:
                     x = jnp.where(row_id + (b - 2 * a) * BLK <= col_id, x, NEG)
-                s_buf[block(b)] = x
+                s_buf[block(b), rows] = x
                 high = jnp.max(x, axis=0, keepdims=True)
                 top = high if top is None else jnp.maximum(top, high)
             total = None
             for b in blocks:
-                e = jnp.exp2((s_buf[block(b)] - top) * exp_scale)
-                s_buf[block(b)] = e
+                e = jnp.exp2((s_buf[block(b), rows] - top) * exp_scale)
+                s_buf[block(b), rows] = e
                 part = jnp.sum(e, axis=0, keepdims=True)
                 total = part if total is None else total + part
             live = jnp.where(first_half, jnp.where(own_live[2 * a], 1.0, 0.0).astype(F32),
                              jnp.where(own_live[2 * a + 1], 1.0, 0.0).astype(F32))
-            scale = live / total
-            for i in range(2):
-                for r, stat in enumerate((top, scale, delta)):
-                    stat_out[h, 4 * r + 2 * a + i:4 * r + 2 * a + i + 1, :] = stat[:, block(i)]
-            for b in blocks:
-                prob = s_buf[block(b)] * scale
+            for r, stat in enumerate((top, live / total, delta_all[:, rows])):
+                for i in range(2):
+                    at = 4 * r + 2 * a + i
+                    stat_out[h, at:at + 1, :] = stat[:, block(i)]
+
+    def grad_part(h):
+        keys, vals = own[h, KEY], own[h, VAL]
+        far_keys = kv_in[h, :, 0].reshape(w * BLK, HD)
+        far_vals = kv_in[h, :, 1].reshape(w * BLK, HD)
+        for a in range(2):
+            near, rows = half(a)
+            grad = own[h, GRD, rows]
+            dp_buf[0:near * BLK] = dot(vals[:near * BLK], grad, both_last)
+            dp_buf[4 * BLK:] = dot(far_vals, grad, both_last)
+            scale, delta = [
+                jnp.concatenate([stat_out[h, at:at + 1, :] for at in (4 * r + 2 * a, 4 * r + 2 * a + 1)], axis=1)
+                for r in (1, 2)]
+            for b in list(range(near)) + [4 + t for t in range(w)]:
+                prob = s_buf[block(b), rows] * scale
                 if b < 4:
                     p_buf[block(b), rows] = prob.astype(BF16)
                 ds_buf[block(b), rows] = (prob * (dp_buf[block(b)] - delta)).astype(BF16)
-            dq = dot(ds_buf[0:nk, rows], keys[:nk], ((0,), (0,)))
-            dq += dot(ds_buf[2 * SL:, rows], far_keys, ((0,), (0,)))
+            dq = dot(ds_buf[0:near * BLK, rows], keys[:near * BLK], ((0,), (0,)))
+            dq += dot(ds_buf[4 * BLK:, rows], far_keys, ((0,), (0,)))
             stage[h, 0, rows] = (dq * inv_root).astype(BF16)
 
     def own_keys(h):
@@ -266,7 +305,7 @@
                 def near(i):
                     return stat_near[h, 4 * r + i:4 * r + i + 1, :]
 
-                row = numbered(t, c_p2, near, lambda i: near(2 + i))
+                row = numbered(t, row_from_even, near, lambda i: near(2 + i))
                 if t == w - 1:
                     row = jnp.where(row_passed[t], stat_far[h, 4 * r:4 * r + 1, :], row)
                 if t == w - 2:
@@ -282,14 +321,11 @@
                 prob = jnp.exp2((sk_buf[block(b), block(t)] - level) * exp_scale) * scale
                 pk_buf[block(b), block(t)] = prob.astype(BF16)
                 dsk_buf[block(b), block(t)] = (prob * (dpk_buf[block(b), block(t)] - delta)).astype(BF16)
+        stage[h, 2] = (part_own[h, 1] + dot(pk_buf[...], grads, nat)).astype(BF16)
+        give(h, 2)
         dk = part_own[h, 0] + dot(dsk_buf[...], queries, nat)
         stage[h, 1] = (dk * inv_root).astype(BF16)
-        stage[h, 2] = (part_own[h, 1] + dot(pk_buf[...], grads, nat)).astype(BF16)
-
-    early = min(LEAD, nh)
-    for h in range(early):
-        for a in (KEY, VAL, QRY, GRD):
-            local_in(h, a).start()
+        give(h, 1)
 
     @pl.when(jnp.logical_not(has_behind))
     def _():
@@ -309,7 +345,7 @@
         for a in (KEY, VAL, QRY, GRD):
             mate_in(h, a).start()
 
-    def start_a(h):
+    def start_keys(h):
         fetched(h, (KEY, VAL))
 
         @when_ahead
@@ -317,6 +353,7 @@
             make_a(h, (KEY, VAL), kv_out)
             keys_a(h).start()
 
+    def start_rows(h):
         fetched(h, (QRY, GRD))
 
         @when_behind
@@ -325,7 +362,8 @@
             rows_a(h).start()
 
     for h in range(early):
-        start_a(h)
+        start_keys(h)
+        start_rows(h)
 
     for h in range(early):
         fetch(h, (OUT,))
@@ -334,81 +372,15 @@
     def _(h):
         fetch(h, (KEY, VAL, QRY, GRD, OUT))
 
-    @pl.loop(0, nh + KEY_LAG)
-    def _(step):
-        @pl.when(step < nh)
-        def _():
-            h = step
-
-            @when_behind
-            def _():
-                keys_a(h).wait_recv()
-
-            @when_ahead
-            def _():
-                make_b(h, (KEY, VAL), kv_in, kv_out, c_m1)
-                keys_b(h).start()
-                rows_a(h).wait_recv()
-
-            @when_behind
-            def _():
-                make_b(h, (QRY, GRD), qg_in, qg_out, c_p2)
-                rows_b(h).start()
-
-        @pl.when(step + early < nh)
-        def _():
-            start_a(step + early)
-
-        @pl.when(step >= KEY_LAG)
-        def _():
-            h = step - KEY_LAG
-
-            @when_ahead
-            def _():
-                rows_b(h).wait_recv()
-                stats_near(h).wait_recv()
-
-            @when_ahead_two
-            def _():
-                stats_far(h).wait_recv()
-
-            key_side(h)
-            for a in (1, 2):
-                local_res(h, a).start()
-                mate_res(h, a).start()
-
-        @pl.when(jnp.logical_and(step >= QUERY_LAG, step < nh + QUERY_LAG))
-        def _():
-            h = step - QUERY_LAG
-            fetched(h, (OUT,))
-
-            @when_behind
-            def _():
-                keys_b(h).wait_recv()
-
-            query_side(h)
-
-            @when_behind
-            def _():
-                stats_near(h).start()
-
-            @when_behind_two
-            def _():
-                stats_far(h).start()
-
-            local_res(h, 0).start()
-            mate_res(h, 0).start()
-            own_keys(h)
-
-    @pl.loop(0, nh)
-    def _(h):
+    def drain(h):
         for a in range(5):
             mate_in(h, a).wait_send()
 
         @when_ahead
         def _():
             keys_a(h).wait_send()
-            keys_b(h).wait_send()
+            for i in range(2):
+                keys_b(h, i).wait_send()
 
         @when_behind
         def _():
@@ -424,6 +396,89 @@
             local_res(h, a).wait()
             mate_res(h, a).wait_send()
             mate_res_arrival(h, a).wait_recv()
+
+    @pl.loop(0, nh + DRAIN_LAG)
+    def _(step):
+        @pl.when(step < nh)
+        def _():
+            h = step
+
+            @when_behind
+            def _():
+                keys_a(h).wait_recv()
+
+            @when_ahead
+            def _():
+                make_b(h, (KEY, VAL), kv_in, kv_out, key_pass)
+                for i in range(2):
+                    keys_b(h, i).start()
+
+        @pl.when(step + early < nh)
+        def _():
+            start_keys(step + early)
+
+        @pl.when(step < nh)
+        def _():
+            h = step
+
+            @when_ahead
+            def _():
+                rows_a(h).wait_recv()
+
+            @when_behind
+            def _():
+                make_b(h, (QRY, GRD), qg_in, qg_out, row_pass)
+                rows_b(h).start()
+
+        @pl.when(step + early < nh)
+        def _():
+            start_rows(step + early)
+
+        @pl.when(jnp.logical_and(step >= KEY_LAG, step < nh + KEY_LAG))
+        def _():
+            h = step - KEY_LAG
+
+            @when_ahead
+            def _():
+                rows_b(h).wait_recv()
+                stats_near(h).wait_recv()
+
+            @when_ahead_two
+            def _():
+                stats_far(h).wait_recv()
+
+            key_side(h)
+
+        @pl.when(jnp.logical_and(step >= QUERY_LAG, step < nh + QUERY_LAG))
+        def _():
+            h = step - QUERY_LAG
+            fetched(h, (OUT,))
+
+            @when_behind
+            def _():
+                keys_b(h, 0).wait_recv()
+
+            soft_part(h)
+
+            @when_behind
+            def _():
+                stats_near(h).start()
+
+            @when_behind_two
+            def _():
+                stats_far(h).start()
+
+            @when_behind
+            def _():
+                keys_b(h, 1).wait_recv()
+
+            grad_part(h)
+            give(h, 0)
+            own_keys(h)
+
+        @pl.when(step >= DRAIN_LAG)
+        def _():
+            drain(step - DRAIN_LAG)
 
 
 def fused(w, owners, queries, key_states, value_states, attn_out, out_grad):
@@ -436,7 +491,7 @@
     return pl.pallas_call(
         functools.partial(kernel, w, nh),
         out_shape=[jax.ShapeDtypeStruct(queries.shape, BF16)] * 3,
-        in_specs=[pl.BlockSpec(memory_space=pltpu.SMEM)] + [anywhere] * 5,
+        in_specs=[anywhere] * 6,
         out_specs=[anywhere] * 3,
         scratch_shapes=[
             pltpu.VMEM((nh, 5, 2 * SL, HD), BF16),
@@ -444,7 +499,7 @@
             stats, stats, stats,
             pltpu.VMEM((nh, 2, 2 * SL, HD), F32),
             pltpu.VMEM((nh, 3, 2 * SL, HD), BF16),
-            pltpu.VMEM(((4 + w) * BLK, SL), F32),
+            pltpu.VMEM(((4 + w) * BLK, 2 * SL), F32),
             pltpu.VMEM(((4 + w) * BLK, SL), F32),
             pltpu.VMEM((2 * SL, 2 * SL), BF16),
             pltpu.VMEM(((4 + w) * BLK, 2 * SL), BF16),
@@ -452,8 +507,10 @@
             pltpu.VMEM((2 * SL, w * BLK), F32),
             pltpu.VMEM((2 * SL, w * BLK), BF16),
             pltpu.VMEM((2 * SL, w * BLK), BF16),
+            pltpu.SMEM(owners.shape, jnp.int32), dma,
             dma((nh, 5)), dma((nh, 5)), dma((nh, 5)),
-        ] + [dma((nh,))] * 12 + [dma((nh, 3))] * 3,
+            dma((nh,)), dma((nh,)), dma((nh, 2)), dma((nh, 2)),
+        ] + [dma((nh,))] * 8 + [dma((nh, 3))] * 3,
         compiler_params=pltpu.CompilerParams(
             collective_id=w - 4, has_side_effects=True, vmem_limit_bytes=56 * 2**20),
         name="slots%d" % w,
@@ -478,12 +535,13 @@
 
 def per_device(queries, key_states, value_states, attn_out, out_grad, owner_ids):
     n_grp, n_seq = lax.axis_size("grp"), lax.axis_size("seq")
-    shard = (owner_ids + n_seq * jnp.arange(n_grp, dtype=jnp.int32)[:, None]).reshape(-1)
-    last = shard + 2 - jnp.logical_or(shard == 0, shard == n_grp * n_seq - 3).astype(jnp.int32)
-    five = (shard[4:] <= last[:-4]).astype(jnp.int32)
-    six = (jnp.pad(shard[5:], (0, 1), constant_values=n_grp * n_seq + 2) <= last[:-4]).astype(jnp.int32)
+    shard = (owner_ids + n_seq * jnp.arange(n_grp, dtype=jnp.int32)[:, None]).reshape(-1, 1, 1)
+    chip = jnp.arange(n_grp * n_seq // 2, dtype=jnp.int32)[None, :]
+    around = 2 * chip + jnp.arange(-3, 5, dtype=jnp.int32)[:, None]
+    m3, m2, m1, e0, o0, p2, p3, p4 = jnp.sum((shard == around).astype(jnp.int32), axis=0)
+    most = jnp.max(jnp.maximum(sum(needs(m1, e0, o0, p2, p3, p4)), sum(needs(p2, o0, e0, m1, m2, m3))))
     return placed(lax.switch(
-        jnp.max(five + six),
+        most - 4,
         [functools.partial(fused, w) for w in (4, 5, 6)],
         owner_ids, queries, key_states, value_states, attn_out, out_grad))
 

time: 71.7 us -> 83.2 us (1.16)
  Pallas kernels: 68.1 us -> 79 us
    pallas_call x1, Pallas kernels: 66.4 us -> 77.3 us  [fused(): pl.pallas_call(functools.partial(kernel, w, nh), out_shape=[jax.ShapeDtyp...]
where the time goes in v4:
time: 83.2 us; the launch traced here: 82.5 us
  Pallas kernels  79 us (95%)
  between operations  1.51 us (2%)
  other arithmetic  0.93 us (1%)
    pallas_call x1, Pallas kernels, fused(): pl.pallas_call(functools.partial(kernel, w, nh), out_shape=[jax.ShapeDtyp...  77.3 us
    pallas_call x1, Pallas kernels, placed(): pl.pallas_call(place, out_shape=[jax.ShapeDtypeStruct(a.shape, a.dtype) f...  1.69 us

profile of v4, /device:TPU:7, one launch (start us, length us, event | category | flops | bytes accessed | tf_op | source)
XLA Modules:
  0.0 82.5 jit_solution(15680629405950117196)
XLA Ops:
  0.6 0.0 copy-start
  0.7 0.7 copy-done
  1.3 0.1 broadcast_add_fusion.1
  1.4 0.1 eq.15
  1.5 0.1 broadcast_add_fusion
  1.6 0.1 convert_reduce_fusion
  1.7 0.6 maximum_reduce_fusion
  3.0 77.6 %conditional.1 = ((bf16[256,2048]{1,0:T(8,128)(2,1)S(1)}, bf16[256,2048]{1,0:T(8,128)(2,1)S(1)}, bf16[256,2048]{1,0:T(8,128)(2,1)S(1)})) conditional(s32[]{:T(128)} %clamp.3, (s32[4,16]{1,0:T(4,128)S(1)}, bf16[256,2048]{1,0:T(8,128)(2,1)}, bf16[256,2048]{1,0:T(8,128)(2,1)}, bf16[256,2048]{1,0:T(8,128)(2,1)}, ...), branch_computations={%region_2.3_spmd, %region_3.4_spmd, %region_4.5_spmd} | conditional | bytes 8 | solution.py:543
  3.0 77.3 %slots5.1 = (bf16[256,2048]{1,0:T(8,128)(2,1)S(1)}, bf16[256,2048]{1,0:T(8,128)(2,1)S(1)}, bf16[256,2048]{1,0:T(8,128)(2,1)S(1)}) custom-call(s32[4,16]{1,0:T(4,128)S(1)} %get-tuple-element.42.owners_in, bf16[256,2048]{1,0:T(8,128)(2,1)} %get-tuple-element.43.q_in, bf16[256,2048]{1,0:T(8,128)(2,1)} %get-tuple-element.44.k_in, ...), custom_call_target="tpu_custom_call" | custom-call | tf_op jit(solution)/shard_map/cond/branch_1_fun/slots5/pallas_call | solution.py:491
  80.6 1.7 %place.1 = (bf16[256,2048]{1,0:T(8,128)(2,1)}, bf16[256,2048]{1,0:T(8,128)(2,1)}, bf16[256,2048]{1,0:T(8,128)(2,1)}) custom-call(bf16[256,2048]{1,0:T(8,128)(2,1)S(1)} %get-tuple-element.60.a, bf16[256,2048]{1,0:T(8,128)(2,1)S(1)} %get-tuple-element.61.b, bf16[256,2048]{1,0:T(8,128)(2,1)S(1)} %get-tuple-element.62.c), custom_call_target="tpu_custom_call" | custom-call | tf_op jit(solution)/shard_map/place/pallas_call | solution.py:530
  (3 shorter events, 0.0 us)
Async XLA Ops:
  0.6 0.7 copy-start
